TPU v7x, 256 devices: a whole 4x4x8 slice. The times are simulated.
256 devices in a mesh: ctx: 8 (over z_hi, y), tile: 8 (over z_lo, core), mp: 4 (over x).
Axes of the slice: x: 4, y: 4, z: 8 (z_hi: 2, z_lo: 4; z = z_hi * 4 + z_lo), core: 2. Of those that a mesh axis runs over, the one named last changes fastest.
Arguments:
- text_embed: bfloat16 [8192, 4096], P('ctx', ('tile', 'mp')), may hold values from -6 to 6
- latents: bfloat16 [16, 64, 512], P('ctx', 'tile'), may hold values from -6 to 6
- down_conv: bfloat16 [72, 256], P(None, 'mp'), may hold values from -0.75 to 0.75
- patch_in: bfloat16 [4096, 4096], P(None, ('tile', 'mp')), may hold values from -0.09375 to 0.09375
- norm_gain: bfloat16 [4096], P(('tile', 'mp')), may hold values from 0.25 to 1.75
- query_weight: bfloat16 [4096, 4096], P(None, ('tile', 'mp')), may hold values from -0.09375 to 0.09375
- key_weight: bfloat16 [4096, 4096], P(None, ('tile', 'mp')), may hold values from -0.09375 to 0.09375
- value_weight: bfloat16 [4096, 4096], P(None, ('tile', 'mp')), may hold values from -0.09375 to 0.09375
- query_gain: float32 [128], replicated, may hold values from 0.5 to 6
- key_gain: float32 [128], replicated, may hold values from 0.5 to 6
- out_weight: bfloat16 [4096, 4096], P(None, ('tile', 'mp')), may hold values from -0.5 to 0.5
- patch_out: bfloat16 [4096, 4096], P(('tile', 'mp')), may hold values from -0.09375 to 0.09375
- up_conv: bfloat16 [2304, 8], replicated, may hold values from -0.125 to 0.125
- span_start: int32 [16], replicated, may hold values from 0 to 7936, as said below
- image_of_slot: int32 [16], replicated, may hold values from 0 to 15, each once
Outputs:
- layer_out: bfloat16 [8192, 4096], P('ctx', ('tile', 'mp'))
- noise_pred: float32 [16, 64, 512], P('ctx', 'tile')
Inputs may be any that keep to these rules, and one draw needn't show every extreme that they name: `span_start`: sorted ascending; each image spans 256 positions, spans do not intersect, the first image starts the document and the last one ends it; spans may cross the boundaries between indices of ctx. `image_of_slot`: each image appears in exactly one slot.
All inputs are finite; a program needn't handle non-finite values.
Results may differ from a plain program's by a relative error of at most 0.04.
Values may be sent and summed in bfloat16 or wider, within the bound.
A program may use at most 128 MiB of HBM per device.

v0:
```python
import jax
import jax.numpy as jnp
from jax import lax
from jax.sharding import PartitionSpec as P

HD = 128
CH = 256
CIN = 8
WL = 64
PATCH = 4
IMG_TOK = 256


EPSILON = 1e-05
NEGATIVE_FILL = -1e30


def padded_2(block, sides, width):
    for axis, dim in sides:
        count = lax.axis_size(axis)
        forward = [(i, i + 1) for i in range(count - 1)]
        backward = [(target, source) for source, target in forward]
        low = lax.ppermute(
            lax.slice_in_dim(block, block.shape[dim] - width, None, axis=dim), axis, forward
        )
        high = lax.ppermute(lax.slice_in_dim(block, 0, width, axis=dim), axis, backward)
        block = jnp.concatenate([low, block, high], axis=dim)
    return block


def rms_scale(values):
    return lax.rsqrt(jnp.mean(values * values, axis=-1, keepdims=True) + EPSILON)


def conv_rows(padded, weight):
    images, padded_height, breadth, channels_in = padded.shape
    height = padded_height - 2
    widened = jnp.pad(padded, ((0, 0), (0, 0), (1, 1), (0, 0)))
    taps = [
        widened[:, row_shift : row_shift + height, col_shift : col_shift + breadth, :]
        for row_shift in range(3)
        for col_shift in range(3)
    ]
    stacked = jnp.concatenate(taps, axis=-1).reshape(images * height * breadth, 9 * channels_in)
    result = jnp.dot(stacked, weight, preferred_element_type=jnp.float32)
    return result.reshape(images, height, breadth, weight.shape[1])


def image_ids(positions, span_start):
    inside = (positions[:, None] >= span_start[None, :]) & (
        positions[:, None] < span_start[None, :] + IMG_TOK
    )
    numbers = jnp.arange(span_start.shape[0], dtype=jnp.int32)
    return jnp.sum(jnp.where(inside, numbers[None, :] + 1, 0), axis=1) - 1


def slot_lookup(image_of_slot):
    numbers = jnp.arange(image_of_slot.shape[0], dtype=jnp.int32)
    matches = image_of_slot[None, :] == numbers[:, None]
    return jnp.sum(jnp.where(matches, numbers[None, :], 0), axis=1)


def shards(
    text_embed,
    latents,
    down_conv,
    patch_in,
    norm_gain,
    query_weight,
    key_weight,
    value_weight,
    query_gain,
    key_gain,
    out_weight,
    patch_out,
    up_conv,
    span_start,
    image_of_slot,
):
    mp_count = lax.axis_size("mp")
    ctx_index = lax.axis_index("ctx")
    seq_rows, slice_width = text_embed.shape
    local_images, band_height, row_width = latents.shape
    image_count = span_start.shape[0]
    quarter_channels = down_conv.shape[1]
    image = latents.reshape(local_images, band_height, WL, CIN)
    padded = padded_2(image, (("tile", 1),), 1)
    activated = jax.nn.silu(conv_rows(padded, down_conv)).astype(jnp.bfloat16)
    band_patches = band_height // PATCH * (WL // PATCH)
    patches = activated.reshape(
        local_images, band_height // PATCH, PATCH, WL // PATCH, PATCH, quarter_channels
    )
    patches = patches.transpose(0, 1, 3, 2, 4, 5).reshape(
        local_images, band_patches, PATCH * PATCH * quarter_channels
    )
    split_in = patch_in.reshape(PATCH * PATCH, mp_count, quarter_channels, slice_width)
    tokens_init = jnp.zeros((local_images, IMG_TOK, slice_width), jnp.float32)
    shard_part = lax.all_gather(patches[None], ("tile", "mp"), axis=0, tiled=True)

    def one_shard(offset, inner):
        weight = lax.dynamic_index_in_dim(split_in, offset % mp_count, 1, keepdims=False)
        weight = weight.reshape(PATCH * PATCH * quarter_channels, slice_width)
        single = lax.dynamic_index_in_dim(shard_part, offset, 0, keepdims=False)
        term = jnp.einsum("ipf,fd->ipd", single, weight, preferred_element_type=jnp.float32)
        row_offset = offset // mp_count * band_patches
        current = lax.dynamic_slice_in_dim(inner, row_offset, band_patches, 1)
        return lax.dynamic_update_slice_in_dim(inner, current + term, row_offset, 1)

    image_tokens = lax.fori_loop(0, shard_part.shape[0], one_shard, tokens_init).astype(
        jnp.bfloat16
    )
    every_token = lax.all_gather(
        image_tokens.reshape(local_images * IMG_TOK, slice_width), "ctx", axis=0, tiled=True
    )
    positions = ctx_index * seq_rows + jnp.arange(seq_rows, dtype=jnp.int32)
    owners = image_ids(positions, span_start)
    safe_owner = jnp.maximum(owners, 0)
    slot_table = slot_lookup(image_of_slot)
    owner_start = jnp.take(span_start, safe_owner)
    source_rows = jnp.take(slot_table, safe_owner) * IMG_TOK + positions - owner_start
    source_rows = jnp.clip(source_rows, 0, image_count * IMG_TOK - 1)
    stream = jnp.where(
        (owners >= 0)[:, None], jnp.take(every_token, source_rows, axis=0), text_embed
    )
    gain_row = norm_gain.reshape(1, slice_width)
    work_owners = image_ids(positions, span_start)
    whole, gain_whole = (
        lax.all_gather(stream, ("tile", "mp"), axis=1, tiled=True),
        lax.all_gather(gain_row, ("tile", "mp"), axis=1, tiled=True),
    )
    widened = whole.astype(jnp.float32)
    normed = (widened * rms_scale(widened) * gain_whole.astype(jnp.float32)).astype(jnp.bfloat16)
    query_raw = jnp.dot(normed, query_weight, preferred_element_type=jnp.float32)
    key_raw = jnp.dot(normed, key_weight, preferred_element_type=jnp.float32)
    value_raw = jnp.dot(normed, value_weight, preferred_element_type=jnp.float32)
    heads_here = query_weight.shape[1] // HD

    def head_norm(raw, gain, factor):
        shaped = raw.reshape(seq_rows, heads_here, HD)
        return (shaped * rms_scale(shaped) * gain * factor).astype(jnp.bfloat16)

    queries = head_norm(query_raw, query_gain, HD ** (-0.5))
    key_rows = head_norm(key_raw, key_gain, 1.0)
    value_rows = value_raw.astype(jnp.bfloat16).reshape(seq_rows, heads_here, HD)
    fold_shard_part = (
        lax.all_gather(key_rows, "ctx", axis=0, tiled=True),
        lax.all_gather(value_rows, "ctx", axis=0, tiled=True),
    )
    key_positions = jnp.arange(fold_shard_part[0].shape[0], dtype=jnp.int32)
    key_part, value_part = fold_shard_part
    key_owners = image_ids(key_positions, span_start)
    visible = (key_positions[None, :] <= positions[:, None]) | (
        key_owners[None, :] == work_owners[:, None]
    ) & (work_owners[:, None] >= 0)
    scores = jnp.einsum("qhd,khd->qhk", queries, key_part, preferred_element_type=jnp.float32)
    scores = jnp.where(visible[:, None, :], scores, NEGATIVE_FILL)
    old_top = jnp.full((seq_rows, heads_here), NEGATIVE_FILL, jnp.float32)
    new_top = jnp.maximum(old_top, jnp.max(scores, axis=2))
    weights = jnp.where(visible[:, None, :], jnp.exp(scores - new_top[:, :, None]), 0.0)
    factor = jnp.exp(old_top - new_top)
    new_sum = jnp.sum(weights, axis=2)
    product = jnp.einsum(
        "qhk,khd->qhd", weights.astype(jnp.bfloat16), value_part, preferred_element_type=jnp.float32
    )
    attended = (
        (product / new_sum[:, :, None]).astype(jnp.bfloat16).reshape(seq_rows, heads_here * HD)
    )
    rows_used = out_weight
    mixed = jnp.dot(
        lax.all_gather(attended, ("tile", "mp"), axis=1, tiled=True),
        rows_used,
        preferred_element_type=jnp.float32,
    )
    work_out = (stream.astype(jnp.float32) + mixed).astype(jnp.bfloat16)
    every_row = lax.all_gather(work_out, "ctx", axis=0, tiled=True)
    slots = ctx_index * local_images + jnp.arange(local_images, dtype=jnp.int32)
    starts = jnp.take(span_start, jnp.take(image_of_slot, slots))
    picked = jax.vmap(
        lambda first_token: lax.dynamic_slice_in_dim(every_row, first_token, IMG_TOK, 0)
    )(starts)
    patch_major = picked.transpose(1, 0, 2).reshape(IMG_TOK * local_images, slice_width)
    rows_used = patch_major
    own_rows = lax.psum_scatter(
        jnp.dot(rows_used, patch_out, preferred_element_type=jnp.float32).astype(jnp.bfloat16),
        ("tile", "mp"),
        scatter_dimension=0,
        tiled=True,
    ).astype(jnp.float32)
    own_active = jax.nn.silu(own_rows).astype(jnp.bfloat16)
    band = lax.all_gather(own_active, "mp", axis=0, tiled=True)
    pixels = band.reshape(band_height // PATCH, WL // PATCH, local_images, PATCH, PATCH, CH)
    pixels = pixels.transpose(2, 0, 3, 1, 4, 5).reshape(local_images, band_height, WL, CH)
    padded_up = padded_2(pixels, (("tile", 1),), 1)
    noise_pred = conv_rows(padded_up, up_conv).reshape(local_images, band_height, WL * CIN)
    return (work_out, noise_pred)


def solution(mesh):
    return jax.shard_map(
        shards,
        mesh=mesh,
        in_specs=(
            P("ctx", ("tile", "mp")),
            P("ctx", "tile", None),
            P(None, "mp"),
            P(None, ("tile", "mp")),
            P(("tile", "mp")),
            P(None, ("tile", "mp")),
            P(None, ("tile", "mp")),
            P(None, ("tile", "mp")),
            P(),
            P(),
            P(None, ("tile", "mp")),
            P(("tile", "mp"), None),
            P(),
            P(),
            P(),
        ),
        out_specs=(P("ctx", ("tile", "mp")), P("ctx", "tile", None)),
        check_vma=False,
    )
```

profile of v0, /device:TPU:1, one launch (start us, length us, event | category | flops | bytes accessed | tf_op | source)
XLA Modules:
  0.0 904.6 jit_solution(7670845394570170660)
XLA Ops:
  8.4 5.1 collective-permute-start.1
  17.7 4.3 concatenate.49
  24.3 92.4 %all-gather.13.cloned.1.call-done = bf16[32,2,32,1024]{3,2,1,0:T(8,128)(2,1)} async-done(((bf16[1,2,32,1024]{3,2,1,0:T(8,128)(2,1)}), bf16[32,2,32,1024]{3,2,1,0:T(8,128)(2,1)}) %all-gather.13.cloned.1.call-update) | async-done | bytes 4194320 | tf_op jit(solution)/shard_map/all_gather | solution.py:98
  116.7 67.5 %while.16 = (s32[]{:T(128)}, f32[2,256,128]{2,1,0:T(8,128)S(1)}, bf16[32,2,32,1024]{3,2,1,0:T(8,128)(2,1)}, bf16[16,4,64,128]{3,2,1,0:T(8,128)(2,1)}, s32[]{:T(1...) while((s32[]{:T(128)}, f32[2,256,128]{2,1,0:T(8,128)S(1)}, ...), condition=%wide.region_3.5_spmd, body=%wide.region_2.4_spmd.sunk | while | flops 16785428 | bytes 983372 | solution.py:109
  186.6 20.0 %compare_and_fusion.1 = (pred[1024]{0:T(1024)(128)(4,1)S(1)}, s32[1024]{0:T(1024)S(1)}) fusion(s32[]{:T(128)} %bitcast.34, s32[]{:T(128)} %bitcast.33, s32[]{:T(128)} %bitcast.32, s32[]{:T(128)} %bitcast.31, s32[]{:T(128)} %bitcast.30, s32[]{:T(128)} %bitcast.29, s32[]{:T(128)} %bitcast.28, s32[]{:T(128)} %bitcast.27, s32[]{:T(128)} %bitcast.26, ...), kind=kLoop, calls=%fused_computation.96 | loop fusion | flops 62464 | bytes 9348 | tf_op jit(solution)/shard_map/jit(_take)/and | solution.py:123
  206.6 39.5 %all-gather.15.cloned.1.call-done = bf16[4096,128]{1,0:T(8,128)(2,1)} async-done(((bf16[512,128]{1,0:T(8,128)(2,1)}), bf16[4096,128]{1,0:T(8,128)(2,1)}) %all-gather.15.cloned.1.call-update) | async-done | bytes 1048592 | tf_op jit(solution)/shard_map/all_gather | solution.py:112
  251.5 62.8 %all-gather.4 = bf16[32,1,128]{2,1,0:T(2,128)(2,1)S(1)} all-gather(bf16[1,1,128]{2,1,0:T(2,128)(2,1)S(1)} %bitcast.172), channel_id=2, replica_groups=mesh['ctx'=8,'tile'=8,'mp'=4] {'tile','mp'}, dimensions={0}, use_global_device_ids=true | all-gather | bytes 8448 | tf_op jit(solution)/shard_map/all_gather | solution.py:129
  314.4 34.7 %all-gather.17.cloned.1.call-done = bf16[1024,4096]{1,0:T(8,128)(2,1)} async-done(((bf16[1024,128]{1,0:T(8,128)(2,1)}), bf16[1024,4096]{1,0:T(8,128)(2,1)}) %all-gather.17.cloned.1.call-update) | async-done | bytes 8388624 | tf_op jit(solution)/shard_map/all_gather | solution.py:128
  349.1 5.1 fusion.8
  354.2 10.5 %fusion.10 = bf16[1024,4096]{1,0:T(8,128)(2,1)} fusion(bf16[1024,4096]{1,0:T(8,128)(2,1)} %all-gather.17.cloned.1.call-done, f32[4096]{0:T(1024)S(1)} %bitcast.170, f32[1024]{0:T(1024)S(1)} %add_rsqrt_fusion.2), kind=kLoop, calls=%fused_computation.22 | loop fusion | flops 16777216 | bytes 16797696 | tf_op jit(solution)/shard_map/convert_element_type | solution.py:132
  364.6 6.4 multiply_reduce_fusion.1
  372.4 6.3 multiply_reduce_fusion
  378.7 6.7 convolution_convert_fusion.1
  385.5 59.4 %all-gather.23.cloned.1.call-done = bf16[8192,128]{0,1:T(8,128)(2,1)} async-done(((bf16[1024,128]{0,1:T(8,128)(2,1)}), bf16[8192,128]{0,1:T(8,128)(2,1)}) %all-gather.23.cloned.1.call-update) | async-done | bytes 2097168 | tf_op jit(solution)/shard_map/all_gather | solution.py:146
  444.9 16.6 %fusion.5 = (f32[1024]{0:T(1024)S(1)}, f32[8192,1024]{1,0:T(8,128)}) fusion(pred[1024]{0:T(1024)(128)(4,1)S(1)} %broadcast_compare_fusion, s32[1024]{0:T(1024)S(1)} %broadcast_add_fusion.1, s32[8192]{0:T(1024)S(1)} %broadcast_add_fusion, s32[1024]{0:T(1024)S(1)} %iota_add_fusion, bf16[8192,128]{0,1:T(8,128)(2,1)} %all-gather.23.cloned.1.call-done, ...), kind=kOutput, calls=%fused_computation.15 | convolution fusion | flops 2198338560 | bytes 36226560 | tf_op jit(solution)/shard_map/qhd,khd->qhk/dot_general | solution.py:155
  461.5 18.4 %fusion.6 = f32[1024]{0:T(1024)S(1)} fusion(f32[8192,1024]{1,0:T(8,128)} %get-tuple-element.237, f32[1024]{0:T(1024)S(1)} %broadcast_maximum_fusion, pred[1024]{0:T(1024)(128)(4,1)S(1)} %broadcast_compare_fusion, s32[1024]{0:T(1024)S(1)} %broadcast_add_fusion.1, s32[8192]{0:T(1024)S(1)} %broadcast_add_fusion, s32[1024]{0:T(1024)S(1)} %iota_add_fusion), kind=kLoop, calls=%fused_computation.16 | loop fusion | flops 67107840 | bytes 33604608 | tf_op jit(solution)/shard_map/reduce_sum | solution.py:161
  480.0 39.2 %all-gather.21.cloned.1.call-done = bf16[8192,128]{1,0:T(8,128)(2,1)} async-done(((bf16[1024,128]{1,0:T(8,128)(2,1)}), bf16[8192,128]{1,0:T(8,128)(2,1)}) %all-gather.21.cloned.1.call-update) | async-done | bytes 2097168 | tf_op jit(solution)/shard_map/all_gather | solution.py:147
  519.2 20.7 %fusion.31 = bf16[1024,1,128]{0,2,1:T(8,128)(2,1)} fusion(bf16[8192,128]{1,0:T(8,128)(2,1)} %all-gather.21.cloned.1.call-done, f32[8192,1024]{1,0:T(8,128)} %get-tuple-element.237, f32[1024]{0:T(1024)S(1)} %broadcast_maximum_fusion, f32[1024]{0:T(1024)S(1)} %fusion.6, s32[1024]{0:T(1024)S(1)} %broadcast_add_fusion.1, s32[1024]{0:T(1024)S(1)} %iota_add_fusion, ...), kind=kOutput, calls=%fused_computation.37 | convolution fusion | flops 2214854656 | bytes 35963904 | tf_op jit(solution)/shard_map/qhk,khd->qhd/dot_general | solution.py:162
  540.0 92.6 %all-gather.25.cloned.1.call-done = bf16[1024,1,4096]{0,2,1:T(8,128)(2,1)} async-done(((bf16[1024,1,128]{0,2,1:T(8,128)(2,1)}), bf16[1024,1,4096]{0,2,1:T(8,128)(2,1)}) %all-gather.25.cloned.1.call-update) | async-done | bytes 8388624 | tf_op jit(solution)/shard_map/all_gather | solution.py:170
  632.5 6.5 fusion.22
  640.7 74.1 %all-gather.19.cloned.1.call-done = bf16[8192,128]{1,0:T(8,128)(2,1)} async-done(((bf16[1024,128]{1,0:T(8,128)(2,1)}), bf16[8192,128]{1,0:T(8,128)(2,1)}) %all-gather.19.cloned.1.call-update) | async-done | bytes 2097168 | tf_op jit(solution)/shard_map/all_gather | solution.py:175
  720.2 142.6 %reduce-scatter.2.cloned.1.call-done = bf16[16,4096]{1,0:T(8,128)(2,1)} async-done(((bf16[512,4096]{1,0:T(8,128)(2,1)}), bf16[16,4096]{1,0:T(8,128)(2,1)}) %reduce-scatter.2.cloned.1.call-update) | async-done | bytes 131088 | tf_op jit(solution)/shard_map/reduce_scatter | solution.py:183
  863.8 9.9 %all_gather.35 = bf16[64,4096]{1,0:T(8,128)(2,1)S(1)} all-gather(bf16[16,4096]{1,0:T(8,128)(2,1)S(1)} %fusion.44), channel_id=1, replica_groups=mesh['ctx'=8,'tile'=8,'mp'=4] {'mp'}, dimensions={0}, use_global_device_ids=true | all-gather | bytes 655360 | tf_op jit(solution)/shard_map/all_gather | solution.py:190
  874.6 11.0 %collective-permute-start.3 = (bf16[2,1,64,256]{3,0,2,1:T(2,128)(2,1)S(1)}, bf16[2,1,64,256]{3,0,2,1:T(2,128)(2,1)S(1)}, u32[]{:S(2)}, u32[]{:S(2)}) collective-permute-start(bf16[2,1,64,256]{3,0,2,1:T(2,128)(2,1)S(1)} %get-tuple-element.189), channel_id=1, source_target_pairs={{4,0},{8,4},{12,8},{16,12},{20,16},{24,20},{28,24},{5,1},{9,5},{13... | collective-permute-start | bytes 196616 | tf_op jit(solution)/shard_map/ppermute | solution.py:26
  (189 shorter events, 105.6 us)
Async XLA Ops:
  7.2 709.8 %copy-start = (bf16[128,4096]{1,0:T(8,128)(2,1)S(1)}, bf16[128,4096]{1,0:T(8,128)(2,1)}, u32[]{:S(2)}) copy-start(bf16[128,4096]{1,0:T(8,128)(2,1)} %param.32) | copy-start | bytes 3145732
  7.2 109.5 %all-gather.13.cloned.1.call-start = ((), (), s32[]{:S(2)}) async-start(), calls=%async_computation.1 | async-start | bytes 4325376 | tf_op jit(solution)/shard_map/all_gather | solution.py:98
  8.4 7.2 collective-permute-start.1
  13.5 3.1 collective-permute-start
  15.6 169.3 %copy-start.2 = (s32[16]{0:T(128)S(1)}, s32[16]{0:T(128)}, u32[]{:S(2)}) copy-start(s32[16]{0:T(128)} %param.35) | copy-start | bytes 196
  15.6 169.5 %copy-start.1 = (s32[16]{0:T(128)S(1)}, s32[16]{0:T(128)}, u32[]{:S(2)}) copy-start(s32[16]{0:T(128)} %param.34) | copy-start | bytes 196
  17.1 234.4 %copy-start.7 = (bf16[128]{0:T(256)(128)(2,1)S(1)}, bf16[128]{0:T(256)(128)(2,1)}, u32[]{:S(2)}) copy-start(bf16[128]{0:T(256)(128)(2,1)} %param.25) | copy-start | bytes 772
  21.9 228.4 %copy-start.6 = (bf16[1024,128]{1,0:T(8,128)(2,1)S(1)}, bf16[1024,128]{1,0:T(8,128)(2,1)}, u32[]{:S(2)}) copy-start(bf16[1024,128]{1,0:T(8,128)(2,1)} %param.21) | copy-start | bytes 786436
  24.2 221.9 %all-gather.15.cloned.1.call-start = ((), (), s32[]{:S(2)}) async-start(), calls=%async_computation.2 | async-start | bytes 1179648 | tf_op jit(solution)/shard_map/all_gather | solution.py:112
  184.9 164.2 %all-gather.17.cloned.1.call-start = ((), (), s32[]{:S(2)}) async-start(), calls=%async_computation.3 | async-start | bytes 8650752 | tf_op jit(solution)/shard_map/all_gather | solution.py:128
  251.4 193.4 %all-gather.23.cloned.1.call-start = ((), (), s32[]{:S(2)}) async-start(), calls=%async_computation.7 | async-start | bytes 2359296 | tf_op jit(solution)/shard_map/all_gather | solution.py:146
  354.2 10.5 %copy-start.4 = (bf16[4096,128]{1,0:T(8,128)(2,1)S(1)}, bf16[4096,128]{1,0:T(8,128)(2,1)}, u32[]{:S(2)}) copy-start(bf16[4096,128]{1,0:T(8,128)(2,1)} %param.27) | copy-start | bytes 3145732
  364.6 6.4 copy-start.8
  364.6 7.8 copy-start.5
  371.9 147.2 %all-gather.21.cloned.1.call-start = ((), (), s32[]{:S(2)}) async-start(), calls=%async_computation.6 | async-start | bytes 2359296 | tf_op jit(solution)/shard_map/all_gather | solution.py:147
  378.7 66.2 %copy-start.11 = (f32[128]{0:T(128)S(1)}, f32[128]{0:T(128)}, u32[]{:S(2)}) copy-start(f32[128]{0:T(128)} %param.29) | copy-start | bytes 1540
  385.4 247.1 %all-gather.25.cloned.1.call-start = ((), (), s32[]{:S(2)}) async-start(), calls=%async_computation.8 | async-start | bytes 8650752 | tf_op jit(solution)/shard_map/all_gather | solution.py:170
  479.9 152.6 %copy-start.3 = (bf16[1024,128]{1,0:T(8,128)(2,1)S(1)}, bf16[1024,128]{1,0:T(8,128)(2,1)}, u32[]{:S(2)}) copy-start(bf16[1024,128]{1,0:T(8,128)(2,1)} %select_select_fusion) | copy-start | bytes 786436
  479.9 152.6 %copy-start.9 = (bf16[4096,128]{1,0:T(8,128)(2,1)S(1)}, bf16[4096,128]{1,0:T(8,128)(2,1)}, u32[]{:S(2)}) copy-start(bf16[4096,128]{1,0:T(8,128)(2,1)} %param.31) | copy-start | bytes 3145732
  539.9 175.0 %all-gather.19.cloned.1.call-start = ((), (), s32[]{:S(2)}) async-start(), calls=%async_computation.4 | async-start | bytes 2359296 | tf_op jit(solution)/shard_map/all_gather | solution.py:175
  639.0 223.8 %reduce-scatter.2.cloned.1.call-start = ((), (), s32[]{:S(2)}) async-start(), calls=%async_computation.5 | async-start | bytes 4325376 | tf_op jit(solution)/shard_map/reduce_scatter | solution.py:183
  874.6 13.4 %collective-permute-start.3 = (bf16[2,1,64,256]{3,0,2,1:T(2,128)(2,1)S(1)}, bf16[2,1,64,256]{3,0,2,1:T(2,128)(2,1)S(1)}, u32[]{:S(2)}, u32[]{:S(2)}) collective-permute-start(bf16[2,1,64,256]{3,0,2,1:T(2,128)(2,1)S(1)} %get-tuple-element.189), channel_id=1, source_target_pairs={{4,0},{8,4},{12,8},{16,12},{20,16},{24,20},{28,24},{5,1},{9,5},{13... | collective-permute-start | bytes 196616 | tf_op jit(solution)/shard_map/ppermute | solution.py:26
  885.6 3.2 collective-permute-start.2
  893.0 2.4 copy-start.10
Sparse Core Ops, SparseCore 0:
  24.4 92.2 all-gather.12
  185.0 61.1 all-gather.14
  251.6 97.4 all-gather.16
  372.0 72.8 all-gather.22
  447.4 71.7 all-gather.20
  540.0 92.4 all-gather.24
  639.1 75.6 all-gather.18
  720.3 142.4 reduce-scatter.1
where the time goes:
time: 907 us; the launch traced here: 905 us
  waiting for transfers between devices  577 us (64%)
  matrix products  104 us (11%)
  blocking collectives  72.7 us (8%)
  other arithmetic  60.3 us (7%)
  local copies, waits for them, and re-layouts  54.3 us (6%)
  starting transfers between devices  20.8 us (2%)
  between operations  14.8 us (2%)
    reduce_scatter x1, waiting for transfers between devices, shards(): lax.psum_scatter(jnp.dot(rows_used, patch_out, preferred_element_type=jnp...  143 us
    all_gather x1, waiting for transfers between devices, shards(): lax.all_gather(attended, ('tile', 'mp'), axis=1, tiled=True)  92.6 us
    all_gather x1, waiting for transfers between devices, shards(): lax.all_gather(patches[None], ('tile', 'mp'), axis=0, tiled=True)  92.4 us
    all_gather x1, waiting for transfers between devices, shards(): every_row = lax.all_gather(work_out, 'ctx', axis=0, tiled=True)  74.1 us
    all_gather x1, blocking collectives, shards(): lax.all_gather(gain_row, ('tile', 'mp'), axis=1, tiled=True)  62.8 us
    all_gather x1, waiting for transfers between devices, shards(): lax.all_gather(key_rows, 'ctx', axis=0, tiled=True)  59.4 us
    all_gather x1, waiting for transfers between devices, shards(): lax.all_gather(image_tokens.reshape(local_images * IMG_TOK, slice_width),...  39.5 us
    all_gather x1, waiting for transfers between devices, shards(): lax.all_gather(value_rows, 'ctx', axis=0, tiled=True)  39.2 us
  transfers between devices with their start and end apart: 12, of which 10 were waited for; matrix products, arithmetic and copies ran while one was open for 8% of the time, Pallas kernels for 0%

commit v1 on v0

v1 whole, which is shorter than its diff:
```python
import functools

import jax
import jax.numpy as jnp
from jax import lax
from jax.experimental import pallas as pl
from jax.experimental.pallas import tpu as pltpu
from jax.sharding import PartitionSpec as P

HD = 128
CH = 256
CIN = 8
PATCH = 4
IMG_TOK = 256
UNIT = 512
EPSILON = 1e-05
NEGATIVE = -1e30
MESH = pl.DeviceIdType.MESH
ANY = pl.BlockSpec(memory_space=pl.ANY)
BF = jnp.bfloat16
F32 = jnp.float32


def remote(src, dst, send, recv, device):
    return pltpu.make_async_remote_copy(
        src_ref=src, dst_ref=dst, send_sem=send, recv_sem=recv, device_id=device, device_id_type=MESH
    )


def barrier(devices):
    sem = pltpu.get_barrier_semaphore()
    for device in devices:
        pl.semaphore_signal(sem, inc=1, device_id=device, device_id_type=MESH)
    pl.semaphore_wait(sem, len(devices))


def coordinates():
    return lax.axis_index("ctx"), lax.axis_index("tile"), lax.axis_index("mp")


class Gather:
    def __init__(self, over, sources, dst, send, recv, local):
        ctx, tile, mp = coordinates()
        self.sources, self.dst, self.send, self.recv, self.local = sources, dst, send, recv, local
        self.pending, self.count = [], 0
        if over == "xz":
            self.size, self.a, self.r, self.core = 4, tile // 2, mp, tile % 2
            self.dev = lambda a, r, core: (ctx, a * 2 + core, r)
            self.slot = lambda a, r, core: (a * 2 + core) * 4 + r
            self.sibling = 1 - self.core
        else:
            self.size, self.a, self.r, self.core = 2, ctx // 4, ctx % 4, 0
            self.dev = lambda a, r, core: (a * 4 + r, tile, mp)
            self.slot = lambda a, r, core: a * 4 + r
            self.sibling = None
        self.right, self.left, self.far = (self.r + 1) % 4, (self.r + 3) % 4, (self.r + 2) % 4

    def partners(self):
        found = [self.dev((self.a + d) % self.size, self.r, self.core) for d in range(1, self.size)]
        found += [self.dev(self.a, self.right, self.core), self.dev(self.a, self.left, self.core)]
        if self.sibling is not None:
            found.append(self.dev(self.a, self.r, self.sibling))
        return found

    def push(self, src, slot, unit, device, half=None):
        dst = self.dst.at[slot, unit]
        which = 0
        if half is not None:
            rows = pl.ds(half * (UNIT // 2), UNIT // 2)
            src, dst, which = src.at[rows], dst.at[rows], half
        copy = remote(src, dst, self.send.at[self.count], self.recv.at[unit, slot, which], device)
        self.count += 1
        copy.start()
        self.pending.append(copy)

    def arrive(self, slot, unit, half=None):
        dst = self.dst.at[slot, unit]
        which = 0
        if half is not None:
            dst, which = dst.at[pl.ds(half * (UNIT // 2), UNIT // 2)], half
        device = self.dev(self.a, self.right, self.core)
        remote(dst, dst, self.send.at[0], self.recv.at[unit, slot, which], device).wait_recv()

    def run(self):
        own = self.slot(self.a, self.r, self.core)
        units = len(self.sources)
        right = self.dev(self.a, self.right, self.core)
        left = self.dev(self.a, self.left, self.core)
        twin = None if self.sibling is None else self.dev(self.a, self.r, self.sibling)
        locals_ = []
        for u, src in enumerate(self.sources):
            for d in range(1, self.size):
                self.push(src, own, u, self.dev((self.a + d) % self.size, self.r, self.core))
            self.push(src, own, u, right)
            self.push(src, own, u, left)
            if twin is not None:
                self.push(src, own, u, twin)
            copy = pltpu.make_async_copy(src, self.dst.at[own, u], self.local.at[u])
            copy.start()
            locals_.append(copy)
        yield
        steps = [(k, u) for k in range(self.size) for u in range(units)]
        for n in range(len(steps) + 2 * units):
            if n < len(steps):
                k, u = steps[n]
                if k > 0:
                    slot = self.slot((self.a + k) % self.size, self.r, self.core)
                    self.arrive(slot, u)
                    src = self.dst.at[slot, u]
                    self.push(src, slot, u, right)
                    self.push(src, slot, u, left)
                    if twin is not None:
                        self.push(src, slot, u, twin)
                    yield
            if 0 <= n - units < len(steps):
                k, u = steps[n - units]
                a = (self.a + k) % self.size
                for ring, target, half in ((self.left, right, 0), (self.right, left, 1)):
                    slot = self.slot(a, ring, self.core)
                    self.arrive(slot, u)
                    self.push(self.dst.at[slot, u], slot, u, target, half)
                    if twin is not None:
                        self.push(self.dst.at[slot, u], slot, u, twin)
                yield
            if 0 <= n - 2 * units < len(steps):
                k, u = steps[n - 2 * units]
                slot = self.slot((self.a + k) % self.size, self.far, self.core)
                self.arrive(slot, u, 0)
                self.arrive(slot, u, 1)
                if twin is not None:
                    self.push(self.dst.at[slot, u], slot, u, twin)
                yield
        if twin is not None:
            for k in range(self.size):
                for ring in (self.r, self.left, self.right, self.far):
                    for u in range(units):
                        self.arrive(self.slot((self.a + k) % self.size, ring, self.sibling), u)
            yield
        for copy in locals_:
            copy.wait()
        for copy in self.pending:
            copy.wait_send()


def interleave(runs):
    runs = list(runs)
    while runs:
        left = []
        for run in runs:
            try:
                next(run)
                left.append(run)
            except StopIteration:
                pass
        runs = left


def gather_sems(over, units):
    slots, sends = (32, 35) if over == "xz" else (8, 9)
    return [
        pltpu.SemaphoreType.DMA((units * sends,)),
        pltpu.SemaphoreType.DMA((units, slots, 2)),
        pltpu.SemaphoreType.DMA((units,)),
    ]


def gather_call(jobs, collective_id):
    flat = [array for _, arrays in jobs for array in arrays]

    def kernel(*refs):
        inputs, refs = refs[: len(flat)], refs[len(flat) :]
        outputs, sems = refs[: len(jobs)], refs[len(jobs) :]
        built, at = [], 0
        for i, (over, arrays) in enumerate(jobs):
            sources = inputs[at : at + len(arrays)]
            at += len(arrays)
            built.append(Gather(over, sources, outputs[i], *sems[3 * i : 3 * i + 3]))
        barrier([device for job in built for device in job.partners()])
        interleave([job.run() for job in built])

    shapes, scratch = [], []
    for over, arrays in jobs:
        slots = 32 if over == "xz" else 8
        shapes.append(jax.ShapeDtypeStruct((slots, len(arrays), UNIT, HD), BF))
        scratch += gather_sems(over, len(arrays))
    return pl.pallas_call(
        kernel,
        out_shape=shapes,
        in_specs=[ANY] * len(flat),
        out_specs=[ANY] * len(jobs),
        scratch_shapes=scratch,
        compiler_params=pltpu.CompilerParams(collective_id=collective_id, has_side_effects=True),
    )(*flat)


def opening_kernel(
    text, patch_out, gain, latents, down, text_all, columns, gains, latents_all, down_all,
    send, recv, local, col_send, col_recv, gain_send, gain_recv, lat_send, lat_recv, down_send, down_recv, own_sem,
):
    ctx, tile, mp = coordinates()
    me = tile * 4 + mp
    job = Gather("ctx", [text.at[u] for u in range(2)], text_all, send, recv, local)
    others = []
    for i in range(1, 32):
        peer = (me + i) % 32
        others.append((ctx, peer // 4, peer % 4))
    barrier(others + job.partners())

    def part(peer):
        return patch_out.at[:, pl.ds(pl.multiple_of(peer * HD, HD), HD)]

    lat_copies, down_copies = [], []
    for i in range(1, 8):
        copy = remote(latents, latents_all.at[tile], lat_send.at[i], lat_recv.at[tile], (ctx, (tile + i) % 8, mp))
        copy.start()
        lat_copies.append(copy)
    for i in range(1, 4):
        copy = remote(down, down_all.at[mp], down_send.at[i], down_recv.at[mp], (ctx, tile, (mp + i) % 4))
        copy.start()
        down_copies.append(copy)
    own = [
        pltpu.make_async_copy(latents, latents_all.at[tile], own_sem.at[0]),
        pltpu.make_async_copy(down, down_all.at[mp], own_sem.at[1]),
        pltpu.make_async_copy(part(me), columns.at[me], own_sem.at[2]),
        pltpu.make_async_copy(gain, gains.at[me], own_sem.at[3]),
    ]
    for copy in own:
        copy.start()
    run = job.run()
    next(run)

    def column_copy(i):
        peer = (me + i) % 32
        device = (ctx, peer // 4, peer % 4)
        return remote(part(peer), columns.at[me], col_send.at[i], col_recv.at[me], device)

    def gain_copy(i):
        peer = (me + i) % 32
        device = (ctx, peer // 4, peer % 4)
        return remote(gain, gains.at[me], gain_send.at[i], gain_recv.at[me], device)

    def start(i, carry):
        column_copy(i).start()
        gain_copy(i).start()
        return carry

    lax.fori_loop(1, 32, start, 0)
    interleave([run])

    def finish(i, carry):
        peer = (me + i) % 32
        device = (ctx, peer // 4, peer % 4)
        column_copy(i).wait_send()
        gain_copy(i).wait_send()
        remote(columns.at[peer], columns.at[peer], col_send.at[i], col_recv.at[peer], device).wait_recv()
        remote(gain, gains.at[peer], gain_send.at[i], gain_recv.at[peer], device).wait_recv()
        return carry

    lax.fori_loop(1, 32, finish, 0)
    for i, copy in enumerate(lat_copies):
        peer = (tile + i + 1) % 8
        copy.wait_send()
        remote(latents, latents_all.at[peer], lat_send.at[0], lat_recv.at[peer], (ctx, peer, mp)).wait_recv()
    for i, copy in enumerate(down_copies):
        peer = (mp + i + 1) % 4
        copy.wait_send()
        remote(down, down_all.at[peer], down_send.at[0], down_recv.at[peer], (ctx, tile, peer)).wait_recv()
    for copy in own:
        copy.wait()


def opening(text, patch_out, gain, latents, down):
    dma = pltpu.SemaphoreType.DMA
    return pl.pallas_call(
        opening_kernel,
        out_shape=[
            jax.ShapeDtypeStruct((8, 2, UNIT, HD), BF),
            jax.ShapeDtypeStruct((32, HD, HD), BF),
            jax.ShapeDtypeStruct((32, 16, HD), BF),
            jax.ShapeDtypeStruct((8,) + latents.shape, BF),
            jax.ShapeDtypeStruct((4,) + down.shape, BF),
        ],
        in_specs=[ANY] * 5,
        out_specs=[ANY] * 5,
        scratch_shapes=gather_sems("ctx", 2)
        + [dma((32,)), dma((32,)), dma((32,)), dma((32,)), dma((8,)), dma((8,)), dma((4,)), dma((4,)), dma((4,))],
        compiler_params=pltpu.CompilerParams(collective_id=1, has_side_effects=True),
    )(text, patch_out, gain, latents, down)


def bands_kernel(up, out, send, recv, high_send, high_recv, low_send, low_recv, own_sem):
    ctx, tile, mp = coordinates()
    me = tile * 4 + mp
    row = tile // 2
    others = []
    for i in range(1, 32):
        peer = (me + i) % 32
        others.append((ctx, peer // 4, peer % 4))
    barrier(others)

    def band(target):
        return up.at[:, pl.ds(pl.multiple_of(target * 32, 32), 32)]

    def above(target):
        return up.at[:, pl.ds(pl.multiple_of(target * 32 - 16, 16), 16)]

    def below(target):
        return up.at[:, pl.ds(pl.multiple_of(target * 32 + 32, 16), 16)]

    spots = {"band": (16, 32), "high": (0, 16), "low": (48, 16)}

    def spot(source, kind):
        first, size = spots[kind]
        return out.at[source, :, pl.ds(first, size)]

    def copies(i):
        peer = (me + i) % 32
        target = peer // 4
        device = (ctx, target, peer % 4)
        return (
            target,
            lambda: remote(band(target), spot(me, "band"), send.at[i], recv.at[me], device),
            lambda: remote(above(target), spot(me, "high"), high_send.at[i], high_recv.at[me], device),
            lambda: remote(below(target), spot(me, "low"), low_send.at[i], low_recv.at[me], device),
        )

    def start(i, carry):
        target, mid, high, low = copies(i)
        mid().start()

        @pl.when((row == 3) & (target > 0))
        def _():
            high().start()

        @pl.when((row == 0) & (target < 7))
        def _():
            low().start()

        return carry

    lax.fori_loop(1, 32, start, 0)
    local = pltpu.make_async_copy(band(tile), spot(me, "band"), own_sem.at[0])
    local.start()

    @pl.when(row == 3)
    def _():
        copy = pltpu.make_async_copy(above(tile), spot(me, "high"), own_sem.at[1])
        copy.start()
        copy.wait()

    @pl.when(row == 0)
    def _():
        copy = pltpu.make_async_copy(below(tile), spot(me, "low"), own_sem.at[2])
        copy.start()
        copy.wait()

    def finish(i, carry):
        target, mid, high, low = copies(i)
        mid().wait_send()

        @pl.when((row == 3) & (target > 0))
        def _():
            high().wait_send()

        @pl.when((row == 0) & (target < 7))
        def _():
            low().wait_send()

        peer = (me + i) % 32
        device = (ctx, target, peer % 4)
        remote(band(tile), spot(peer, "band"), send.at[i], recv.at[peer], device).wait_recv()

        @pl.when((peer // 8 == 3) & (tile > 0))
        def _():
            remote(spot(peer, "high"), spot(peer, "high"), high_send.at[i], high_recv.at[peer], device).wait_recv()

        @pl.when((peer // 8 == 0) & (tile < 7))
        def _():
            remote(spot(peer, "low"), spot(peer, "low"), low_send.at[i], low_recv.at[peer], device).wait_recv()

        return carry

    lax.fori_loop(1, 32, finish, 0)
    local.wait()


def bands(up):
    return pl.pallas_call(
        bands_kernel,
        out_shape=jax.ShapeDtypeStruct((32, 2, 64, HD), BF),
        in_specs=[ANY],
        out_specs=ANY,
        scratch_shapes=[pltpu.SemaphoreType.DMA((32,))] * 6 + [pltpu.SemaphoreType.DMA((3,))],
        compiler_params=pltpu.CompilerParams(collective_id=2, has_side_effects=True),
    )(up)


def silu(v):
    return v / (1.0 + jnp.exp(-v))


def windows(latents_all):
    grid = latents_all.reshape(8, 2, 8, 512).transpose(1, 0, 2, 3).reshape(2, 64, 512)
    wide = jnp.pad(grid, ((0, 0), (1, 1), (8, 32)))
    before = wide[:, :, 0:512].reshape(2, 66, 16, 32)[..., :8]
    middle = wide[:, :, 8:520].reshape(2, 66, 16, 32)
    after = wide[:, :, 40:552].reshape(2, 66, 16, 32)[..., :8]
    joined = jnp.concatenate([before, middle, after], axis=-1)
    rows = [joined[:, k : k + 61 : 4] for k in range(6)]
    return jnp.concatenate(rows, axis=-1).reshape(UNIT, 288)


def tokens_kernel(w_ref, down_ref, patch_ref, out_ref, total):
    px = pl.program_id(0)
    pr, pc = px // 4, px % 4
    row = lax.broadcasted_iota(jnp.int32, (288, 72), 0)
    col = lax.broadcasted_iota(jnp.int32, (288, 72), 1)
    hit = ((col // 24 + pr) * 6 + (col // 8) % 3 + pc) * 8 + col % 8
    pick = jnp.where(row == hit, 1.0, 0.0).astype(BF)
    weight = jnp.dot(pick, down_ref[...], preferred_element_type=F32).astype(BF)
    act = silu(jnp.dot(w_ref[...], weight, preferred_element_type=F32)).astype(BF)
    term = jnp.dot(act, patch_ref[...], preferred_element_type=F32)

    @pl.when(px == 0)
    def _():
        total[...] = term

    @pl.when(px > 0)
    def _():
        total[...] += term

    @pl.when(px == 15)
    def _():
        out_ref[...] = total[...].astype(BF)


def tokens_of(w, down, patch_in):
    return pl.pallas_call(
        tokens_kernel,
        grid=(16,),
        out_shape=jax.ShapeDtypeStruct((UNIT, HD), BF),
        in_specs=[
            pl.BlockSpec((UNIT, 288), lambda i: (0, 0)),
            pl.BlockSpec((72, CH), lambda i: (0, 0)),
            pl.BlockSpec((CH, HD), lambda i: (i, 0)),
        ],
        out_specs=pl.BlockSpec((UNIT, HD), lambda i: (0, 0)),
        scratch_shapes=[pltpu.VMEM((UNIT, HD), F32)],
    )(w, down, patch_in)


TILE = 256


def qkv_kernel(x_ref, gain_ref, wq_ref, wk_ref, wv_ref, qg_ref, kg_ref, q_ref, kv_ref):
    squares = jnp.zeros((TILE, HD), F32)
    for i in range(32):
        part = x_ref[i, 0].astype(F32)
        squares += part * part
    scale = lax.rsqrt(jnp.sum(squares, axis=1, keepdims=True) * (1.0 / 4096.0) + EPSILON)
    normed = jnp.concatenate(
        [
            (x_ref[i, 0].astype(F32) * scale * gain_ref[:, i * HD : (i + 1) * HD].astype(F32)).astype(BF)
            for i in range(32)
        ],
        axis=1,
    )

    def head(weight, gain, factor):
        raw = jnp.dot(normed, weight, preferred_element_type=F32)
        mean = jnp.mean(raw * raw, axis=1, keepdims=True)
        return (raw * lax.rsqrt(mean + EPSILON) * gain * factor).astype(BF)

    q_ref[0] = head(wq_ref[...], qg_ref[...], HD**-0.5)
    kv_ref[0, 0] = head(wk_ref[...], kg_ref[...], 1.0)
    kv_ref[0, 1] = jnp.dot(normed, wv_ref[...], preferred_element_type=F32).astype(BF)


def qkv_of(x, gain, wq, wk, wv, qg, kg):
    units = x.shape[1]
    per = UNIT // TILE
    weight = pl.BlockSpec((4096, HD), lambda i: (0, 0))
    small = pl.BlockSpec((1, HD), lambda i: (0, 0))
    return pl.pallas_call(
        qkv_kernel,
        grid=(units * per,),
        out_shape=[
            jax.ShapeDtypeStruct((units, UNIT, HD), BF),
            jax.ShapeDtypeStruct((units, 2, UNIT, HD), BF),
        ],
        in_specs=[
            pl.BlockSpec((32, 1, TILE, HD), lambda i: (0, i // per, i % per, 0)),
            pl.BlockSpec((1, 4096), lambda i: (0, 0)),
            weight,
            weight,
            weight,
            small,
            small,
        ],
        out_specs=[
            pl.BlockSpec((1, TILE, HD), lambda i: (i // per, i % per, 0)),
            pl.BlockSpec((1, 2, TILE, HD), lambda i: (i // per, 0, i % per, 0)),
        ],
        compiler_params=pltpu.CompilerParams(vmem_limit_bytes=40 * 1024 * 1024),
    )(x, gain, wq, wk, wv, qg, kg)


def attention_kernel(top_ref, slot_ref, q_ref, lim_t_ref, lim_i_ref, kv_ref, out_ref):
    tile = pl.program_id(0)
    q = q_ref[...]
    cols = lax.broadcasted_iota(jnp.int32, (TILE, 1024), 1)

    def step(carry, k, v, limit):
        top, total, acc = carry
        s = lax.dot_general(q, k, (((1,), (1,)), ((), ())), preferred_element_type=F32)
        s = jnp.where(cols < limit, s, NEGATIVE)
        new = jnp.maximum(top, jnp.max(s, axis=1, keepdims=True))
        w = jnp.exp(s - new)
        factor = jnp.exp(top - new)
        total = total * factor + jnp.sum(w, axis=1, keepdims=True)
        acc = acc * factor + jnp.dot(w.astype(BF), v, preferred_element_type=F32)
        return new, total, acc

    def text_step(n, carry):
        k = jnp.concatenate([kv_ref[2 * n, 0], kv_ref[2 * n + 1, 0]], axis=0)
        v = jnp.concatenate([kv_ref[2 * n, 1], kv_ref[2 * n + 1, 1]], axis=0)
        return step(carry, k, v, lim_t_ref[...] - n * 1024)

    def image_step(n, carry):
        ks, vs = [], []
        for u in range(4):
            slot = slot_ref[n * 4 + u]
            rows = pl.ds(pl.multiple_of((slot % 2) * IMG_TOK, IMG_TOK), IMG_TOK)
            ks.append(kv_ref[slot // 2, 2, rows])
            vs.append(kv_ref[slot // 2, 3, rows])
        return step(carry, jnp.concatenate(ks, axis=0), jnp.concatenate(vs, axis=0), lim_i_ref[...] - n * 1024)

    carry = (jnp.full((TILE, 1), NEGATIVE, F32), jnp.zeros((TILE, 1), F32), jnp.zeros((TILE, HD), F32))
    carry = lax.fori_loop(0, (top_ref[1, tile] + 1023) // 1024, image_step, carry)
    carry = lax.fori_loop(0, (top_ref[0, tile] + 1023) // 1024, text_step, carry)
    _, total, acc = carry
    out_ref[...] = (acc / total).astype(BF)


def attention(tops, slots, q, lim_t, lim_i, kv):
    rows = q.shape[0]
    grid_spec = pltpu.PrefetchScalarGridSpec(
        num_scalar_prefetch=2,
        grid=(rows // TILE,),
        in_specs=[
            pl.BlockSpec((TILE, HD), lambda i, *_: (i, 0)),
            pl.BlockSpec((TILE, 1), lambda i, *_: (i, 0)),
            pl.BlockSpec((TILE, 1), lambda i, *_: (i, 0)),
            pl.BlockSpec((8, 4, UNIT, HD), lambda i, *_: (0, 0, 0, 0)),
        ],
        out_specs=pl.BlockSpec((TILE, HD), lambda i, *_: (i, 0)),
    )
    return pl.pallas_call(
        attention_kernel,
        grid_spec=grid_spec,
        out_shape=jax.ShapeDtypeStruct((rows, HD), BF),
        compiler_params=pltpu.CompilerParams(vmem_limit_bytes=48 * 1024 * 1024),
    )(tops, slots, q, lim_t, lim_i, kv)


def project_kernel(x_ref, w_ref, stream_ref, out_ref):
    x = jnp.concatenate([x_ref[i, 0] for i in range(32)], axis=1)
    mixed = jnp.dot(x, w_ref[...], preferred_element_type=F32)
    out_ref[0] = (stream_ref[0].astype(F32) + mixed).astype(BF)


def project(x, w, stream):
    per = UNIT // TILE
    row_block = pl.BlockSpec((1, TILE, HD), lambda i: (i // per, i % per, 0))
    return pl.pallas_call(
        project_kernel,
        grid=(2 * per,),
        out_shape=jax.ShapeDtypeStruct((2, UNIT, HD), BF),
        in_specs=[
            pl.BlockSpec((32, 1, TILE, HD), lambda i: (0, i // per, i % per, 0)),
            pl.BlockSpec((4096, HD), lambda i: (0, 0)),
            row_block,
        ],
        out_specs=row_block,
        compiler_params=pltpu.CompilerParams(vmem_limit_bytes=32 * 1024 * 1024),
    )(x, w, stream)


def expand_kernel(x_ref, w_ref, out_ref):
    x = jnp.concatenate([x_ref[i, 0] for i in range(32)], axis=1)
    out_ref[...] = silu(jnp.dot(x, w_ref[...], preferred_element_type=F32)).astype(BF)


def expand(x, w):
    per = UNIT // TILE
    return pl.pallas_call(
        expand_kernel,
        grid=(per,),
        out_shape=jax.ShapeDtypeStruct((UNIT, HD), BF),
        in_specs=[
            pl.BlockSpec((32, 1, TILE, HD), lambda i: (0, 0, i, 0)),
            pl.BlockSpec((4096, HD), lambda i: (0, 0)),
        ],
        out_specs=pl.BlockSpec((TILE, HD), lambda i: (i, 0)),
        compiler_params=pltpu.CompilerParams(vmem_limit_bytes=32 * 1024 * 1024),
    )(x, w)


def up_weights(up_conv):
    taps = up_conv.reshape(9, CH, CIN).transpose(1, 0, 2).reshape(CH, 72)
    row = lax.broadcasted_iota(jnp.int32, (72, 36 * HD), 0)
    col = lax.broadcasted_iota(jnp.int32, (72, 36 * HD), 1)
    cell, inner = col // HD, col % HD
    a, b = cell // 6 - inner // 32, cell % 6 - (inner // 8) % 4
    inside = (a >= 0) & (a <= 2) & (b >= 0) & (b <= 2)
    pick = jnp.where(inside & (row == (a * 3 + b) * 8 + inner % 8), 1.0, 0.0).astype(BF)
    return jnp.dot(taps, pick, preferred_element_type=F32).astype(BF)


def up_kernel(edge_ref, g_ref, w_ref, out_ref):
    first, last = edge_ref[0], edge_ref[1]
    inner = lax.broadcasted_iota(jnp.int32, (2, 32, CH), 1)
    sums = [jnp.zeros((64, HD), F32) for _ in range(3)]
    for wr in range(6):
        pr, start = ((3, 0) if wr == 0 else (0, 32) if wr == 5 else (wr - 1, 16))
        for wc in range(6):
            pc = 3 if wc == 0 else 0 if wc == 5 else wc - 1
            px = pr * 4 + pc
            a = jnp.concatenate(
                [g_ref[2 * px, :, start : start + 32], g_ref[2 * px + 1, :, start : start + 32]], axis=-1
            )
            if wr == 0:
                a = jnp.where((inner < 16) & (first == 1), jnp.zeros_like(a), a)
            if wr == 5:
                a = jnp.where((inner >= 16) & (last == 1), jnp.zeros_like(a), a)
            cell = wr * 6 + wc
            term = jnp.dot(
                a.reshape(64, CH), w_ref[:, cell * HD : (cell + 1) * HD], preferred_element_type=F32
            )
            which = 0 if wc == 0 else 2 if wc == 5 else 1
            sums[which] = sums[which] + term
    column = lax.broadcasted_iota(jnp.int32, (64, HD), 0) % 16
    blank = jnp.zeros((1, HD), F32)
    from_left = jnp.concatenate([blank, sums[0][:63]], axis=0)
    from_right = jnp.concatenate([sums[2][1:], blank], axis=0)
    out_ref[...] = (
        sums[1] + jnp.where(column == 0, 0.0, from_left) + jnp.where(column == 15, 0.0, from_right)
    )


def up_block(edges, g, w):
    whole = pl.BlockSpec(memory_space=pltpu.VMEM)
    return pl.pallas_call(
        up_kernel,
        out_shape=jax.ShapeDtypeStruct((64, HD), F32),
        in_specs=[pl.BlockSpec(memory_space=pltpu.SMEM), whole, whole],
        out_specs=whole,
        compiler_params=pltpu.CompilerParams(vmem_limit_bytes=32 * 1024 * 1024),
    )(edges, g, w)


def shards(
    text_embed,
    latents,
    down_conv,
    patch_in,
    norm_gain,
    query_weight,
    key_weight,
    value_weight,
    query_gain,
    key_gain,
    out_weight,
    patch_out,
    up_conv,
    span_start,
    image_of_slot,
):
    ctx, tile = lax.axis_index("ctx"), lax.axis_index("tile")
    images = jnp.arange(16, dtype=jnp.int32)
    before = span_start - images * IMG_TOK
    is_slot = image_of_slot[None, :] == images[:, None]
    slot_of = jnp.sum(jnp.where(is_slot, images[None, :], 0), axis=1)

    text_all, columns, gains, latents_all, down_all = opening(
        text_embed.reshape(2, UNIT, HD),
        patch_out,
        jnp.broadcast_to(norm_gain[None, :], (16, HD)),
        latents.reshape(16, 512),
        jnp.pad(down_conv, ((0, 8), (0, 64))),
    )
    down = jnp.concatenate([down_all[i, :72, :64] for i in range(4)], axis=1)
    gain = gains[:, 0, :].reshape(1, 4096)

    text_rows = ctx * UNIT + jnp.arange(UNIT, dtype=jnp.int32)
    seen = jnp.sum((before[None, :] <= text_rows[:, None]).astype(jnp.int32), axis=1)
    text = jnp.take(text_all.reshape(8192, HD), text_rows + IMG_TOK * seen, axis=0, mode="clip")
    image = tokens_of(windows(latents_all), down, patch_in)

    (x_all,) = gather_call([("xz", [text, image])], 3)
    q, kv = qkv_of(
        x_all, gain, query_weight, key_weight, value_weight, query_gain.reshape(1, HD), key_gain.reshape(1, HD)
    )
    (kv_all,) = gather_call([("ctx", [kv[0, 0], kv[0, 1], kv[1, 0], kv[1, 1]])], 4)

    slots = ctx * 2 + jnp.arange(2, dtype=jnp.int32)
    here = slots[:, None] == images[None, :]
    own_image = jnp.sum(jnp.where(here, image_of_slot[None, :], 0), axis=1)
    own_before = jnp.sum(jnp.where(own_image[:, None] == images[None, :], before[None, :], 0), axis=1)
    spread = lambda pair: jnp.broadcast_to(pair[:, None], (2, IMG_TOK)).reshape(UNIT)
    lim_t = jnp.concatenate([text_rows + 1, spread(own_before)])
    lim_i = jnp.concatenate([seen * IMG_TOK, spread((own_image + 1) * IMG_TOK)])
    tops = jnp.stack([jnp.max(lim_t.reshape(4, TILE), axis=1), jnp.max(lim_i.reshape(4, TILE), axis=1)])
    attended = attention(tops, slot_of, q.reshape(1024, HD), lim_t[:, None], lim_i[:, None], kv_all)

    (mixed_all,) = gather_call([("xz", [attended[:UNIT], attended[UNIT:]])], 5)
    work = project(mixed_all, out_weight, jnp.stack([text, image]))
    rows_all, work_all = gather_call([("xz", [work[1]]), ("ctx", [work[0], work[1]])], 6)
    up = expand(rows_all, columns.reshape(4096, HD))
    grid = bands(up.reshape(2, IMG_TOK, HD))
    edges = jnp.stack([(tile == 0).astype(jnp.int32), (tile == 7).astype(jnp.int32)])
    cells = up_block(edges, grid, up_weights(up_conv))
    noise_pred = cells.reshape(2, 2, 16, 4, 32).transpose(0, 1, 3, 2, 4).reshape(2, 8, 512)

    positions = ctx * 1024 + jnp.arange(1024, dtype=jnp.int32)
    started = (span_start[None, :] <= positions[:, None]).astype(jnp.int32)
    passed = jnp.sum((span_start[None, :] + IMG_TOK <= positions[:, None]).astype(jnp.int32), axis=1)
    inside = jnp.sum(started, axis=1) > passed
    now = passed[:, None] == images[None, :]
    slot = jnp.sum(jnp.where(now, slot_of[None, :], 0), axis=1)
    start = jnp.sum(jnp.where(now, span_start[None, :], 0), axis=1)
    row = positions - passed * IMG_TOK
    text_source = row // UNIT * 1024 + row % UNIT
    image_source = slot // 2 * 1024 + UNIT + slot % 2 * IMG_TOK + positions - start
    layer_out = jnp.take(
        work_all.reshape(8192, HD), jnp.where(inside, image_source, text_source), axis=0, mode="clip"
    )
    return layer_out, noise_pred


def solution(mesh):
    return jax.shard_map(
        shards,
        mesh=mesh,
        in_specs=(
            P("ctx", ("tile", "mp")),
            P("ctx", "tile", None),
            P(None, "mp"),
            P(None, ("tile", "mp")),
            P(("tile", "mp")),
            P(None, ("tile", "mp")),
            P(None, ("tile", "mp")),
            P(None, ("tile", "mp")),
            P(),
            P(),
            P(None, ("tile", "mp")),
            P(("tile", "mp"), None),
            P(),
            P(),
            P(),
        ),
        out_specs=(P("ctx", ("tile", "mp")), P("ctx", "tile", None)),
        check_vma=False,
    )
```

time: 907 us -> 383 us (0.42)
  waiting for transfers between devices: 577 us -> 0 us
  Pallas kernels: 0 us -> 324 us
  matrix products: 104 us -> 1.46 us
  blocking collectives: 72.7 us -> 0 us
  other arithmetic: 60.3 us -> 2.11 us
  starting transfers between devices: 20.8 us -> 0 us
  between operations: 14.8 us -> 1.2 us
    all_gather x7 -> x0, waiting for transfers between devices: 432 us -> none  [the longest x1 92.6 us: shards(): lax.all_gather(attended, ('tile', 'mp'), axis=1, tiled=True)]
    pallas_call x0 -> x12, Pallas kernels: none -> 324 us  [the longest x4 218 us: gather_call(): pl.pallas_call(kernel, out_shape=shapes, in_specs=[ANY] * len(flat), out_...]
    reduce_scatter x1 -> x0, waiting for transfers between devices: 143 us -> none  [shards(): lax.psum_scatter(jnp.dot(rows_used, patch_out, preferred_element_type=jnp...]
    dot_general x41 -> x1, matrix products: 104 us -> 1.46 us  [up_weights(): return jnp.dot(taps, pick, preferred_element_type=F32).astype(BF)]
    all_gather x2 -> x0, blocking collectives: 72.7 us -> none  [the longest x1 62.8 us: shards(): lax.all_gather(gain_row, ('tile', 'mp'), axis=1, tiled=True)]
    dynamic_slice x32 -> x0, local copies, waits for them, and re-layouts: 31.3 us -> none  [one_shard(): lax.dynamic_index_in_dim(split_in, offset % mp_count, 1, keepdims=False)]
    reduce_sum x5 -> x6, other arithmetic: 23.9 us -> 0.76 us  [the longest x1 0.18 us: shards(): own_image = jnp.sum(jnp.where(here, image_of_slot[None, :], 0), axis=1)]
    ppermute x4 -> x0, starting transfers between devices: 20 us -> none  [the longest x2 16.2 us: padded_2(): lax.ppermute(lax.slice_in_dim(block, 0, width, axis=dim), axis, backward)]
  transfers between devices with their start and end apart: 12 -> 0, of which waited for: 10 -> 0; matrix products, arithmetic and copies ran while one was open for 8% -> 0% of each run, Pallas kernels for 0% -> 0%
where the time goes in v1:
time: 383 us; the launch traced here: 380 us
  Pallas kernels  324 us (85%)
  local copies, waits for them, and re-layouts  51 us (13%)
    pallas_call x4, Pallas kernels, gather_call(): pl.pallas_call(kernel, out_shape=shapes, in_specs=[ANY] * len(flat), out_...  218 us
    pallas_call x1, Pallas kernels, opening(): pl.pallas_call(opening_kernel, out_shape=[jax.ShapeDtypeStruct((8, 2, UNI...  46.2 us
    slice x12, local copies, waits for them, and re-layouts, windows(): rows = [joined[:, k:k + 61:4] for k in range(6)]  21.1 us
    pallas_call x1, Pallas kernels, bands(): pl.pallas_call(bands_kernel, out_shape=jax.ShapeDtypeStruct((32, 2, 64, H...  18.3 us
    pallas_call x1, Pallas kernels, tokens_of(): pl.pallas_call(tokens_kernel, grid=(16,), out_shape=jax.ShapeDtypeStruct(...  14.3 us
    unnamed x45, local copies, waits for them, and re-layouts  12.8 us
    pallas_call x1, Pallas kernels, attention(): pl.pallas_call(attention_kernel, grid_spec=grid_spec, out_shape=jax.Shape...  11 us
    pallas_call x1, Pallas kernels, qkv_of(): pl.pallas_call(qkv_kernel, grid=(units * per,), out_shape=[jax.ShapeDtype...  9.94 us

profile of v1, /device:TPU:1, one launch (start us, length us, event | category | flops | bytes accessed | tf_op | source)
XLA Modules:
  0.0 380.2 jit_solution(11766053436124614445)
XLA Ops:
  3.3 46.2 %shard_map.158 = (bf16[8,2,512,128]{3,2,1,0:T(8,128)(2,1)}, bf16[32,128,128]{2,1,0:T(8,128)(2,1)}, bf16[32,16,128]{2,1,0:T(8,128)(2,1)}, bf16[8,16,512]{2,1,0:T(8,128)(2,1)}, bf16[4,80,128]{2,1,0:T(8,128)(2,1)}) custom-call(bf16[2,512,128]{2,1,0:T(8,128)(2,1)} %bitcast.88, bf16[128,4096]{1,0:T(8,128)(2,1)} %patch_out.1, ...), custom_call_target="tpu_custom_call" | custom-call | tf_op jit(solution)/shard_map/pallas_call | solution.py:274
  51.3 3.2 slice.78
  54.7 3.3 slice.79
  58.3 3.3 slice.80
  61.8 3.3 slice.81
  65.4 3.3 slice.82
  68.9 3.3 slice.83
  74.4 14.3 %shard_map.159.refs_1_ = bf16[512,128]{1,0:T(8,128)(2,1)} custom-call(bf16[512,288]{1,0:T(8,128)(2,1)} %bitcast.80, bf16[72,256]{1,0:T(8,128)(2,1)} %pad_maximum_fusion.2.down_ref, bf16[4096,128]{1,0:T(8,128)(2,1)} %patch_ref.1), custom_call_target="tpu_custom_call" | custom-call | tf_op jit(solution)/shard_map/pallas_call | solution.py:438
  88.8 1.9 gather_fusion
  90.7 54.6 %shard_map.160.x_ref = bf16[32,2,512,128]{3,2,1,0:T(8,128)(2,1)} custom-call(bf16[512,128]{1,0:T(8,128)(2,1)} %gather_fusion, bf16[512,128]{1,0:T(8,128)(2,1)} %shard_map.159.refs_1_), custom_call_target="tpu_custom_call" | custom-call | tf_op jit(solution)/shard_map/pallas_call | solution.py:186
  146.2 3.4 copy-done.2
  149.6 9.9 %shard_map.161 = (bf16[2,512,128]{2,1,0:T(8,128)(2,1)S(1)}, bf16[2,2,512,128]{3,2,1,0:T(8,128)(2,1)S(1)}) custom-call(bf16[32,2,512,128]{3,2,1,0:T(8,128)(2,1)S(1)} %copy-done.2, bf16[1,4096]{1,0:T(2,128)(2,1)S(1)} %slice_bitcast_fusion.10.gain_ref, bf16[4096,128]{1,0:T(8,128)(2,1)S(1)} %copy-done.6, bf16[4096,128]{1,0:T(8,128)(2,1)S(1)} %copy-done.7, ...), custom_call_target="tpu_custom_call" | custom-call | tf_op jit(solution)/shard_map/pallas_call | solution.py:484
  160.4 42.1 %shard_map.162.kv_ref = bf16[8,4,512,128]{3,2,1,0:T(8,128)(2,1)} custom-call(bf16[512,128]{1,0:T(8,128)(2,1)} %get-tuple-element.27.refs_0_, bf16[512,128]{1,0:T(8,128)(2,1)} %get-tuple-element.26.refs_1_, bf16[512,128]{1,0:T(8,128)(2,1)} %get-tuple-element.25.refs_2_, bf16[512,128]{1,0:T(8,128)(2,1)} %get-tuple-element.24.refs_3_), custom_call_target="tpu_custom_call" | custom-call | tf_op jit(solution)/shard_map/pallas_call | solution.py:186
  204.1 2.2 copy-done.3
  206.3 11.0 %shard_map.163 = bf16[1024,128]{1,0:T(8,128)(2,1)S(1)} custom-call(s32[2,4]{1,0:T(2,128)S(1)} %pad_add_fusion.2.top_ref, s32[16]{0:T(128)S(1)} %select_reduce_fusion.2.slot_ref, bf16[1024,128]{1,0:T(8,128)(2,1)S(1)} %bitcast.76, s32[1024,1]{1,0:T(8,128)S(1)} %copy.56.lim_t_ref, s32[1024,1]{1,0:T(8,128)S(1)} %copy.57.lim_i_ref, ...), custom_call_target="tpu_custom_call" | custom-call | tf_op jit(solution)/shard_map/pallas_call | solution.py:558
  218.1 58.2 %shard_map.164.x_ref = bf16[32,2,512,128]{3,2,1,0:T(8,128)(2,1)} custom-call(bf16[512,128]{1,0:T(8,128)(2,1)} %get-tuple-element.31.refs_0_, bf16[512,128]{1,0:T(8,128)(2,1)} %get-tuple-element.30.refs_1_), custom_call_target="tpu_custom_call" | custom-call | tf_op jit(solution)/shard_map/pallas_call | solution.py:186
  276.4 3.4 copy-done.1
  279.7 3.5 shard_map.165
  284.0 63.4 %shard_map.166 = (bf16[32,1,512,128]{3,2,1,0:T(8,128)(2,1)}, bf16[8,2,512,128]{3,2,1,0:T(8,128)(2,1)}) custom-call(bf16[512,128]{1,0:T(8,128)(2,1)} %get-tuple-element.29.refs_0_.refs_2_, bf16[512,128]{1,0:T(8,128)(2,1)} %get-tuple-element.28.refs_1_, bf16[512,128]{1,0:T(8,128)(2,1)} %get-tuple-element.29.refs_0_.refs_2_), custom_call_target="tpu_custom_call" | custom-call | tf_op jit(solution)/shard_map/pallas_call | solution.py:186
  347.4 2.2 copy-done.4
  349.6 1.8 shard_map.167
  352.0 18.3 %shard_map.168.g_ref = bf16[32,2,64,128]{3,2,1,0:T(8,128)(2,1)} custom-call(bf16[2,256,128]{2,1,0:T(8,128)(2,1)} %bitcast.75), custom_call_target="tpu_custom_call" | custom-call | tf_op jit(solution)/shard_map/pallas_call | solution.py:388
  370.4 1.5 fusion.w_ref
  374.2 6.0 %gather_fusion.1 = bf16[1024,128]{1,0:T(8,128)(2,1)} fusion(bf16[8192,128]{1,0:T(8,128)(2,1)} %bitcast.79, s32[1024]{0:T(1024)S(1)} %broadcast_clamp_fusion), kind=kCustom, calls=%fused_computation.1 | custom fusion | bytes 528384 | tf_op jit(solution)/shard_map/jit(_take)/gather | solution.py:735
  (102 shorter events, 15.2 us)
Async XLA Ops:
  0.6 369.8 %copy-start = (bf16[2304,8]{0,1:T(8,128)(2,1)S(1)}, bf16[2304,8]{0,1:T(8,128)(2,1)}, u32[]{:S(2)}) copy-start(bf16[2304,8]{0,1:T(8,128)(2,1)} %param.27) | copy-start | bytes 110596
  68.9 4.7 %copy-start.17 = (bf16[4,80,128]{2,1,0:T(8,128)(2,1)S(1)}, bf16[4,80,128]{2,1,0:T(8,128)(2,1)}, u32[]{:S(2)}) copy-start(bf16[4,80,128]{2,1,0:T(8,128)(2,1)} %get-tuple-element.13) | copy-start | bytes 245764
  72.5 16.2 %copy-start.18 = (s32[16]{0:T(128)S(1)}, s32[16]{0:T(128)}, u32[]{:S(2)}) copy-start(s32[16]{0:T(128)} %param.28) | copy-start | bytes 196
  72.5 16.3 %copy-start.16 = (bf16[8,2,512,128]{3,2,1,0:T(8,128)(2,1)S(1)}, bf16[8,2,512,128]{3,2,1,0:T(8,128)(2,1)}, u32[]{:S(2)}) copy-start(bf16[8,2,512,128]{3,2,1,0:T(8,128)(2,1)} %get-tuple-element.11) | copy-start | bytes 6291460
  90.7 55.5 %copy-start.6 = (bf16[4096,128]{1,0:T(8,128)(2,1)S(1)}, bf16[4096,128]{1,0:T(8,128)(2,1)}, u32[]{:S(2)}) copy-start(bf16[4096,128]{1,0:T(8,128)(2,1)} %wq_ref.1) | copy-start | bytes 3145732
  90.7 55.5 %copy-start.7 = (bf16[4096,128]{1,0:T(8,128)(2,1)S(1)}, bf16[4096,128]{1,0:T(8,128)(2,1)}, u32[]{:S(2)}) copy-start(bf16[4096,128]{1,0:T(8,128)(2,1)} %wk_ref.1) | copy-start | bytes 3145732
  90.7 55.5 %copy-start.8 = (bf16[4096,128]{1,0:T(8,128)(2,1)S(1)}, bf16[4096,128]{1,0:T(8,128)(2,1)}, u32[]{:S(2)}) copy-start(bf16[4096,128]{1,0:T(8,128)(2,1)} %wv_ref.1) | copy-start | bytes 3145732
  90.7 55.5 %copy-start.12 = (f32[128]{0:T(128)S(1)}, f32[128]{0:T(128)}, u32[]{:S(2)}) copy-start(f32[128]{0:T(128)} %param.23) | copy-start | bytes 1540
  90.7 55.5 %copy-start.13 = (f32[128]{0:T(128)S(1)}, f32[128]{0:T(128)}, u32[]{:S(2)}) copy-start(f32[128]{0:T(128)} %param.24) | copy-start | bytes 1540
  146.2 3.4 copy-start.2
  160.4 42.2 %copy-start.19 = (s32[16]{0:T(128)S(1)}, s32[16]{0:T(128)}, u32[]{:S(2)}) copy-start(s32[16]{0:T(128)} %param.29) | copy-start | bytes 196
  204.1 2.2 copy-start.3
  218.1 58.2 %copy-start.14 = (bf16[512,128]{1,0:T(8,128)(2,1)S(1)}, bf16[512,128]{1,0:T(8,128)(2,1)}, u32[]{:S(2)}) copy-start(bf16[512,128]{1,0:T(8,128)(2,1)} %shard_map.159.refs_1_) | copy-start | bytes 393220
  218.1 58.2 %copy-start.15 = (bf16[512,128]{1,0:T(8,128)(2,1)S(1)}, bf16[512,128]{1,0:T(8,128)(2,1)}, u32[]{:S(2)}) copy-start(bf16[512,128]{1,0:T(8,128)(2,1)} %gather_fusion) | copy-start | bytes 393220
  218.1 58.3 %copy-start.9 = (bf16[4096,128]{1,0:T(8,128)(2,1)S(1)}, bf16[4096,128]{1,0:T(8,128)(2,1)}, u32[]{:S(2)}) copy-start(bf16[4096,128]{1,0:T(8,128)(2,1)} %w_ref.1) | copy-start | bytes 3145732
  276.4 3.4 copy-start.1
  279.7 67.7 %copy-start.10 = (bf16[32,128,128]{2,1,0:T(8,128)(2,1)S(1)}, bf16[32,128,128]{2,1,0:T(8,128)(2,1)}, u32[]{:S(2)}) copy-start(bf16[32,128,128]{2,1,0:T(8,128)(2,1)} %get-tuple-element.19) | copy-start | bytes 3145732
  347.4 2.2 copy-start.4
  351.4 0.7 copy-start.11
  370.4 1.6 copy-start.5

commit v2 on v1

v2 whole, which is shorter than its diff:
```python
import functools

import jax
import jax.numpy as jnp
from jax import lax
from jax.experimental import pallas as pl
from jax.experimental.pallas import tpu as pltpu
from jax.sharding import PartitionSpec as P

HD = 128
CH = 256
CIN = 8
PATCH = 4
IMG_TOK = 256
UNIT = 512
EPSILON = 1e-05
NEGATIVE = -1e30
MESH = pl.DeviceIdType.MESH
ANY = pl.BlockSpec(memory_space=pl.ANY)
BF = jnp.bfloat16
F32 = jnp.float32


def remote(src, dst, send, recv, device):
    return pltpu.make_async_remote_copy(
        src_ref=src, dst_ref=dst, send_sem=send, recv_sem=recv, device_id=device, device_id_type=MESH
    )


def barrier(devices):
    sem = pltpu.get_barrier_semaphore()
    for device in devices:
        pl.semaphore_signal(sem, inc=1, device_id=device, device_id_type=MESH)
    pl.semaphore_wait(sem, len(devices))


def coordinates():
    return lax.axis_index("ctx"), lax.axis_index("tile"), lax.axis_index("mp")


class Gather:
    def __init__(self, over, sources, dst, send, recv, local):
        ctx, tile, mp = coordinates()
        self.dst, self.send, self.recv, self.local = dst, send, recv, local
        self.rows = dst.shape[2]
        parts = dst.shape[1] // len(sources)
        self.sources = [
            source.at[pl.ds(part * self.rows, self.rows)] for source in sources for part in range(parts)
        ]
        self.pending, self.count = [], 0
        if over != "ctx":
            a = tile // 2
            self.a, self.r, self.core = a, mp, tile % 2
            self.dev = lambda a, r, core: (ctx, a * 2 + core, r)
            if over == "xz":
                self.slot = lambda a, r, core: (a * 2 + core) * 4 + r
            else:
                self.slot = lambda a, r, core: a * 2 + core
            self.sibling = 1 - self.core
            near = a + 1 - 2 * (a % 2)
            cross = 2 - a // 2
            self.order = [a, near, cross, 3 * (1 - a // 2)]
            self.onward = [None, 3 - a, near, near]
            self.middle = (a == 1) | (a == 2)
            self.inner, self.outer = 1 + a % 2, near
            self.others = [(a + d) % 4 for d in range(1, 4)]
        else:
            a = ctx // 4
            self.a, self.r, self.core = a, ctx % 4, 0
            self.dev = lambda a, r, core: (a * 4 + r, tile, mp)
            self.slot = lambda a, r, core: a * 4 + r
            self.sibling = None
            self.order = [a, 1 - a]
            self.middle = None
            self.inner = 1 - a
            self.others = [1 - a]
        self.right, self.left, self.far = (self.r + 1) % 4, (self.r + 3) % 4, (self.r + 2) % 4

    def partners(self):
        found = [self.dev(a, self.r, self.core) for a in self.others]
        found += [self.dev(self.a, self.right, self.core), self.dev(self.a, self.left, self.core)]
        if self.sibling is not None:
            found.append(self.dev(self.a, self.r, self.sibling))
        return found

    def push(self, src, slot, unit, device, half=None, when=None):
        dst = self.dst.at[slot, unit]
        which = 0
        if half is not None:
            rows = pl.ds(half * (self.rows // 2), self.rows // 2)
            src, dst, which = src.at[rows], dst.at[rows], half
        count = self.count
        self.count += 1
        make = lambda: remote(src, dst, self.send.at[count], self.recv.at[unit, slot, which], device)
        self.pending.append((make, when))
        if when is None:
            make().start()
        else:
            pl.when(when)(lambda: make().start())

    def arrive(self, slot, unit, half=None):
        dst = self.dst.at[slot, unit]
        which = 0
        if half is not None:
            dst, which = dst.at[pl.ds(half * (self.rows // 2), self.rows // 2)], half
        device = self.dev(self.a, self.right, self.core)
        remote(dst, dst, self.send.at[0], self.recv.at[unit, slot, which], device).wait_recv()

    def run(self):
        own = self.slot(self.a, self.r, self.core)
        units = len(self.sources)
        right = self.dev(self.a, self.right, self.core)
        left = self.dev(self.a, self.left, self.core)
        twin = None if self.sibling is None else self.dev(self.a, self.r, self.sibling)
        locals_ = []
        for u, src in enumerate(self.sources):
            self.push(src, own, u, self.dev(self.inner, self.r, self.core))
            if self.middle is not None:
                self.push(src, own, u, self.dev(self.outer, self.r, self.core), when=self.middle)
            self.push(src, own, u, right)
            self.push(src, own, u, left)
            if twin is not None:
                self.push(src, own, u, twin)
            copy = pltpu.make_async_copy(src, self.dst.at[own, u], self.local.at[u])
            copy.start()
            locals_.append(copy)
        yield
        steps = [(k, u) for k in range(len(self.order)) for u in range(units)]
        for n in range(len(steps) + 2 * units):
            if n < len(steps):
                k, u = steps[n]
                if k > 0:
                    slot = self.slot(self.order[k], self.r, self.core)
                    self.arrive(slot, u)
                    src = self.dst.at[slot, u]
                    if self.middle is not None:
                        device = self.dev(self.onward[k], self.r, self.core)
                        self.push(src, slot, u, device, when=self.middle)
                    self.push(src, slot, u, right)
                    self.push(src, slot, u, left)
                    if twin is not None:
                        self.push(src, slot, u, twin)
                    yield
            if 0 <= n - units < len(steps):
                k, u = steps[n - units]
                a = self.order[k]
                for ring, target, half in ((self.left, right, 0), (self.right, left, 1)):
                    slot = self.slot(a, ring, self.core)
                    self.arrive(slot, u)
                    self.push(self.dst.at[slot, u], slot, u, target, half)
                    if twin is not None:
                        self.push(self.dst.at[slot, u], slot, u, twin)
                yield
            if 0 <= n - 2 * units < len(steps):
                k, u = steps[n - 2 * units]
                slot = self.slot(self.order[k], self.far, self.core)
                self.arrive(slot, u, 0)
                self.arrive(slot, u, 1)
                if twin is not None:
                    self.push(self.dst.at[slot, u], slot, u, twin)
                yield
        if twin is not None:
            for k in range(len(self.order)):
                for ring in (self.r, self.left, self.right, self.far):
                    for u in range(units):
                        self.arrive(self.slot((self.a + k) % 4, ring, self.sibling), u)
            yield
        self.close(locals_)

    def close(self, locals_):
        for copy in locals_:
            copy.wait()
        for make, when in self.pending:
            if when is None:
                make().wait_send()
            else:
                pl.when(when)(lambda make=make: make().wait_send())

    def run_column(self):
        own = self.slot(self.a, self.r, self.core)
        units = len(self.sources)
        twin = self.dev(self.a, self.r, self.sibling)
        locals_ = []
        for u, src in enumerate(self.sources):
            self.push(src, own, u, self.dev(self.inner, self.r, self.core))
            self.push(src, own, u, self.dev(self.outer, self.r, self.core), when=self.middle)
            self.push(src, own, u, twin)
            copy = pltpu.make_async_copy(src, self.dst.at[own, u], self.local.at[u])
            copy.start()
            locals_.append(copy)
        for u in range(units):
            for k in range(1, 4):
                slot = self.slot(self.order[k], self.r, self.core)
                self.arrive(slot, u)
                src = self.dst.at[slot, u]
                self.push(src, slot, u, self.dev(self.onward[k], self.r, self.core), when=self.middle)
                self.push(src, slot, u, twin)
            locals_[u].wait()
            for k in range(4):
                self.arrive(self.slot(self.order[k], self.r, self.sibling), u)
            yield u
        self.close([])


def interleave(runs):
    runs = list(runs)
    while runs:
        left = []
        for run in runs:
            try:
                next(run)
                left.append(run)
            except StopIteration:
                pass
        runs = left


def gather_sems(over, units):
    slots, sends = {"xz": (32, 37), "ctx": (8, 12), "z": (8, 12)}[over]
    return [
        pltpu.SemaphoreType.DMA((units * sends,)),
        pltpu.SemaphoreType.DMA((units, slots, 2)),
        pltpu.SemaphoreType.DMA((units,)),
    ]


class Spread:
    def __init__(self, src, dst, send, recv, local):
        self.ctx, tile, mp = coordinates()
        self.me = tile * 4 + mp
        self.src, self.dst, self.send, self.recv, self.local = src, dst, send, recv, local

    def peer(self, i):
        peer = (self.me + i) % 32
        return peer, (self.ctx, peer // 4, peer % 4)

    def partners(self):
        return [self.peer(i)[1] for i in range(1, 32)]

    def copy(self, i):
        return remote(self.src, self.dst.at[self.me], self.send.at[i], self.recv.at[self.me], self.peer(i)[1])

    def run(self):
        own = pltpu.make_async_copy(self.src, self.dst.at[self.me], self.local.at[0])
        own.start()

        def start(i, carry):
            self.copy(i).start()
            return carry

        def finish(i, carry):
            self.copy(i).wait_send()
            peer, device = self.peer(i)
            remote(self.src, self.dst.at[peer], self.send.at[i], self.recv.at[peer], device).wait_recv()
            return carry

        yield
        lax.fori_loop(1, 32, start, 0)
        yield
        lax.fori_loop(1, 32, finish, 0)
        own.wait()


def spread_sems():
    return [pltpu.SemaphoreType.DMA((32,)), pltpu.SemaphoreType.DMA((32,)), pltpu.SemaphoreType.DMA((1,))]


class Weights:
    def __init__(self, out_weight, patch_out, out_all, patch_all, out_send, out_recv, patch_send, patch_recv, local):
        self.ctx, self.tile, self.mp = coordinates()
        self.core, self.z = self.tile % 2, self.tile // 2
        self.out_weight, self.patch_out, self.out_all, self.patch_all = out_weight, patch_out, out_all, patch_all
        self.out_send, self.out_recv, self.patch_send, self.patch_recv = out_send, out_recv, patch_send, patch_recv
        self.local = local

    def mates(self):
        found = []
        for i in range(1, 8):
            core, mp = (self.core + i // 4) % 2, (self.mp + i) % 4
            found.append((core, mp, (self.ctx, self.z * 2 + core, mp)))
        return found

    def partners(self):
        return [device for _, _, device in self.mates()]

    def columns(self, core, mp):
        return self.patch_out.at[:, pl.ds(pl.multiple_of(mp * 1024 + core * 512, 512), 512)]

    def run(self):
        own = self.core * 4 + self.mp
        copies = []
        for i, (core, mp, device) in enumerate(self.mates()):
            if i < 3:
                copies.append(
                    remote(
                        self.out_weight.at[:, mp], self.out_all.at[self.mp], self.out_send.at[i],
                        self.out_recv.at[self.mp], device,
                    )
                )
            copies.append(
                remote(
                    self.columns(core, mp), self.patch_all.at[own], self.patch_send.at[i],
                    self.patch_recv.at[own], device,
                )
            )
        here = [
            pltpu.make_async_copy(self.out_weight.at[:, self.mp], self.out_all.at[self.mp], self.local.at[0]),
            pltpu.make_async_copy(self.columns(self.core, self.mp), self.patch_all.at[own], self.local.at[1]),
        ]
        for copy in copies + here:
            copy.start()
        yield
        yield
        for i, (core, mp, device) in enumerate(self.mates()):
            slot = core * 4 + mp
            if i < 3:
                dst = self.out_all.at[mp]
                remote(dst, dst, self.out_send.at[0], self.out_recv.at[mp], device).wait_recv()
            dst = self.patch_all.at[slot]
            remote(dst, dst, self.patch_send.at[0], self.patch_recv.at[slot], device).wait_recv()
        for copy in copies:
            copy.wait_send()
        for copy in here:
            copy.wait()


def weight_sems():
    return [pltpu.SemaphoreType.DMA((n,)) for n in (3, 4, 7, 8, 2)]


def merge(groups):
    return [device for group in groups for device in group]


def gather_call(jobs, collective_id, gain=None, weights=None, parts=1):
    flat = [array for _, arrays in jobs for array in arrays]
    extra = ([gain] if gain is not None else []) + (list(weights) if weights is not None else [])
    inputs_in = flat + extra

    def kernel(*refs):
        inputs, refs = refs[: len(inputs_in)], refs[len(inputs_in) :]
        outputs, sems = refs[: len(shapes)], refs[len(shapes) :]
        built, at = [], 0
        for i, (over, arrays) in enumerate(jobs):
            sources = inputs[at : at + len(arrays)]
            at += len(arrays)
            built.append(Gather(over, sources, outputs[i], *sems[3 * i : 3 * i + 3]))
        rest = sems[3 * len(jobs) :]
        if gain is not None:
            built.append(Spread(inputs[at], outputs[len(jobs)], *rest))
        if weights is not None:
            built.append(Weights(inputs[at], inputs[at + 1], outputs[len(jobs)], outputs[len(jobs) + 1], *rest))
        barrier(merge(job.partners() for job in built))
        interleave([job.run() for job in built])

    shapes, scratch = [], []
    for over, arrays in jobs:
        slots = 32 if over == "xz" else 8
        rows, width = arrays[0].shape
        shapes.append(jax.ShapeDtypeStruct((slots, len(arrays) * parts, rows // parts, width), BF))
        scratch += gather_sems(over, len(arrays) * parts)
    if gain is not None:
        shapes.append(jax.ShapeDtypeStruct((32,) + gain.shape, BF))
        scratch += spread_sems()
    if weights is not None:
        shapes += [jax.ShapeDtypeStruct((4, 8, HD, HD), BF), jax.ShapeDtypeStruct((8, HD, 512), BF)]
        scratch += weight_sems()
    return pl.pallas_call(
        kernel,
        out_shape=shapes,
        in_specs=[ANY] * len(inputs_in),
        out_specs=[ANY] * len(shapes),
        scratch_shapes=scratch,
        compiler_params=pltpu.CompilerParams(collective_id=collective_id, has_side_effects=True),
    )(*inputs_in)


def opening_kernel(
    latents, down, latents_all, down_all, lat_send, lat_recv, down_send, down_recv, own_sem
):
    ctx, tile, mp = coordinates()
    tiles = [((tile + i) % 8) for i in range(1, 8)]
    mps = [((mp + i) % 4) for i in range(1, 4)]
    barrier([(ctx, t, mp) for t in tiles] + [(ctx, tile, m) for m in mps])
    copies = []
    for i, t in enumerate(tiles):
        copies.append(remote(latents, latents_all.at[tile], lat_send.at[i], lat_recv.at[tile], (ctx, t, mp)))
    for i, m in enumerate(mps):
        copies.append(remote(down, down_all.at[mp], down_send.at[i], down_recv.at[mp], (ctx, tile, m)))
    own = [
        pltpu.make_async_copy(latents, latents_all.at[tile], own_sem.at[0]),
        pltpu.make_async_copy(down, down_all.at[mp], own_sem.at[1]),
    ]
    for copy in copies + own:
        copy.start()
    for t in tiles:
        remote(latents, latents_all.at[t], lat_send.at[0], lat_recv.at[t], (ctx, t, mp)).wait_recv()
    for m in mps:
        remote(down, down_all.at[m], down_send.at[0], down_recv.at[m], (ctx, tile, m)).wait_recv()
    for copy in copies:
        copy.wait_send()
    for copy in own:
        copy.wait()


def opening(latents, down):
    dma = pltpu.SemaphoreType.DMA
    return pl.pallas_call(
        opening_kernel,
        out_shape=[
            jax.ShapeDtypeStruct((8,) + latents.shape, BF),
            jax.ShapeDtypeStruct((4,) + down.shape, BF),
        ],
        in_specs=[ANY] * 2,
        out_specs=[ANY] * 2,
        scratch_shapes=[dma((7,)), dma((8,)), dma((3,)), dma((4,)), dma((2,))],
        compiler_params=pltpu.CompilerParams(collective_id=1, has_side_effects=True),
    )(latents, down)


MIX = 256


def mix_kernel(
    image, text, w_ref, image_stream, text_stream, image_out, text_out,
    blocks, outgoing, incoming, send, recv, local, part_send, part_recv,
):
    ctx, tile, mp = coordinates()
    units = blocks.shape[1]
    job = Gather("z", [image, text], blocks, send, recv, local)
    rings = [(mp + 1) % 4, (mp + 3) % 4, (mp + 2) % 4]
    barrier(merge([job.partners(), [(ctx, tile, rings[2])]]))

    def settle(u):
        for i, ring in enumerate(rings):
            dst = incoming.at[ring, u]
            remote(dst, dst, part_send.at[0, 0], part_recv.at[ring, u], (ctx, tile, ring)).wait_recv()
        stream, out, row = (image_stream, image_out, u * MIX) if u < 2 else (text_stream, text_out, u * MIX - UNIT)
        total = stream[row : row + MIX].astype(F32) + kept[u]
        for ring in rings:
            total = total + incoming[ring, u].astype(F32)
        out[row : row + MIX] = total.astype(BF)

    kept, copies = {}, []
    for u in job.run_column():
        x = jnp.concatenate([blocks[t, u] for t in range(8)], axis=1)
        for i, ring in enumerate(rings):
            outgoing[i, u] = jnp.dot(x, w_ref[ring], preferred_element_type=F32).astype(BF)
            copy = remote(
                outgoing.at[i, u], incoming.at[mp, u], part_send.at[i, u], part_recv.at[mp, u], (ctx, tile, ring)
            )
            copy.start()
            copies.append(copy)
        kept[u] = jnp.dot(x, w_ref[mp], preferred_element_type=F32)
        if u > 0:
            settle(u - 1)
    settle(units - 1)
    for copy in copies:
        copy.wait_send()


def mix(image, text, w, image_stream, text_stream):
    dma = pltpu.SemaphoreType.DMA
    units = 2 * UNIT // MIX
    vmem = pl.BlockSpec(memory_space=pltpu.VMEM)
    return pl.pallas_call(
        mix_kernel,
        out_shape=[jax.ShapeDtypeStruct((UNIT, HD), BF)] * 2,
        in_specs=[ANY, ANY, vmem, vmem, vmem],
        out_specs=[vmem, vmem],
        scratch_shapes=[
            pltpu.VMEM((8, units, MIX, HD), BF),
            pltpu.VMEM((3, units, MIX, HD), BF),
            pltpu.VMEM((4, units, MIX, HD), BF),
        ]
        + gather_sems("z", units)
        + [dma((3, units)), dma((4, units))],
        compiler_params=pltpu.CompilerParams(
            collective_id=2, has_side_effects=True, vmem_limit_bytes=32 * 1024 * 1024
        ),
    )(image, text, w, image_stream, text_stream)


def up_kernel(
    image, text, w_ref, up_ref, image_work, text_work, cells_ref,
    blocks, product, terms, grid, above, below,
    image_send, image_recv, image_local, text_send, text_recv, text_local,
    block_send, block_recv, twin_send, twin_recv, term_send, term_recv, grid_send, grid_recv, edge_send, edge_recv,
    own_sem,
):
    ctx, tile, mp = coordinates()
    z, core = tile // 2, tile % 2
    jobs = [
        Gather("ctx", [image], image_work, image_send, image_recv, image_local),
        Gather("ctx", [text], text_work, text_send, text_recv, text_local),
    ]
    me = tile * 4 + mp
    group = []
    for i in range(1, 32):
        peer = (me + i) % 32
        group.append((ctx, peer // 4, peer % 4))
    barrier(merge([group, jobs[0].partners()]))
    rings = [(mp + 1) % 4, (mp + 3) % 4, (mp + 2) % 4]
    twin = (ctx, z * 2 + 1 - core, mp)
    own = core * 4 + mp
    copies = []

    def go(copy):
        copy.start()
        copies.append(copy)

    for i, ring in enumerate(rings):
        go(remote(image, blocks.at[own], block_send.at[i], block_recv.at[mp], (ctx, tile, ring)))
    go(remote(image, blocks.at[own], twin_send.at[mp], twin_recv.at[mp], twin))
    mine = pltpu.make_async_copy(image, blocks.at[own], own_sem.at[0])
    mine.start()
    runs = [job.run() for job in jobs]
    for run in runs:
        next(run)
    for ring in rings:
        dst = blocks.at[core * 4 + ring]
        remote(dst, dst, block_send.at[0], block_recv.at[ring], (ctx, tile, ring)).wait_recv()
        go(remote(dst, dst, twin_send.at[ring], twin_recv.at[ring], twin))
    mine.wait()
    for ring in range(4):
        dst = blocks.at[(1 - core) * 4 + ring]
        remote(dst, dst, twin_send.at[0], twin_recv.at[ring], twin).wait_recv()
    for s in range(2):
        x = jnp.concatenate([blocks[i, s * IMG_TOK : (s + 1) * IMG_TOK] for i in range(8)], axis=1)
        part = jnp.dot(x, w_ref[...].reshape(1024, 512), preferred_element_type=F32).astype(BF)
        product[:, s] = part.reshape(8, 32, 512)
    tiles = [(tile + i) % 8 for i in (2, 6, 4, 1, 7, 3, 5)]
    for i, t in enumerate(tiles):
        go(remote(product.at[t], terms.at[tile], term_send.at[i], term_recv.at[tile], (ctx, t, mp)))
    mine = pltpu.make_async_copy(product.at[tile], terms.at[tile], own_sem.at[1])
    mine.start()
    for run in runs:
        next(run)
    for t in tiles:
        dst = terms.at[t]
        remote(dst, dst, term_send.at[0], term_recv.at[t], (ctx, t, mp)).wait_recv()
    mine.wait()
    for c in range(2):
        total = terms[c].astype(F32)
        for k in range(1, 4):
            total = total + terms[2 * k + c].astype(F32)
        grid[mp, :, :, c * 512 : (c + 1) * 512] = silu(total).astype(BF)

    for i, ring in enumerate(rings):
        go(remote(grid.at[mp], grid.at[mp], grid_send.at[i], grid_recv.at[mp], (ctx, tile, ring)))
    down_edge = (mp == 3) & (tile < 7)
    up_edge = (mp == 0) & (tile > 0)
    down_copies = [
        lambda m=m: remote(
            grid.at[mp, :, pl.ds(16, 16)], above, edge_send.at[m], edge_recv.at[0], (ctx, (tile + 1) % 8, m)
        )
        for m in range(4)
    ]
    up_copies = [
        lambda m=m: remote(
            grid.at[mp, :, pl.ds(0, 16)], below, edge_send.at[m], edge_recv.at[1], (ctx, (tile + 7) % 8, m)
        )
        for m in range(4)
    ]

    @pl.when(down_edge)
    def _():
        for make in down_copies:
            make().start()

    @pl.when(up_edge)
    def _():
        for make in up_copies:
            make().start()

    @pl.when(tile == 0)
    def _():
        above[...] = jnp.zeros_like(above)

    @pl.when(tile == 7)
    def _():
        below[...] = jnp.zeros_like(below)

    for ring in rings:
        dst = grid.at[ring]
        remote(dst, dst, grid_send.at[0], grid_recv.at[ring], (ctx, tile, ring)).wait_recv()

    @pl.when(tile > 0)
    def _():
        remote(above, above, edge_send.at[0], edge_recv.at[0], (ctx, tile, rings[0])).wait_recv()

    @pl.when(tile < 7)
    def _():
        remote(below, below, edge_send.at[0], edge_recv.at[1], (ctx, tile, rings[0])).wait_recv()

    sums = [jnp.zeros((64, HD), F32) for _ in range(3)]
    for wr in range(6):
        for wc in range(6):
            pc = 3 if wc == 0 else 0 if wc == 5 else wc - 1
            lanes = slice(pc * CH, (pc + 1) * CH)
            if wr == 0:
                a = jnp.concatenate([above[:, :, lanes], grid[3, :, 0:16, lanes]], axis=1)
            elif wr == 5:
                a = jnp.concatenate([grid[0, :, 16:32, lanes], below[:, :, lanes]], axis=1)
            else:
                a = grid[wr - 1, :, :, lanes]
            cell = wr * 6 + wc
            term = jnp.dot(
                a.reshape(64, CH), up_ref[:, cell * HD : (cell + 1) * HD], preferred_element_type=F32
            )
            which = 0 if wc == 0 else 2 if wc == 5 else 1
            sums[which] = sums[which] + term
    column = lax.broadcasted_iota(jnp.int32, (64, HD), 0) % 16
    blank = jnp.zeros((1, HD), F32)
    from_left = jnp.concatenate([blank, sums[0][:63]], axis=0)
    from_right = jnp.concatenate([sums[2][1:], blank], axis=0)
    cells_ref[...] = (
        sums[1] + jnp.where(column == 0, 0.0, from_left) + jnp.where(column == 15, 0.0, from_right)
    )
    interleave(runs)
    for copy in copies:
        copy.wait_send()

    @pl.when(down_edge)
    def _():
        for make in down_copies:
            make().wait_send()

    @pl.when(up_edge)
    def _():
        for make in up_copies:
            make().wait_send()


def up_block(image, text, w, up_w):
    dma = pltpu.SemaphoreType.DMA
    vmem = pl.BlockSpec(memory_space=pltpu.VMEM)
    work = jax.ShapeDtypeStruct((8, 1, UNIT, HD), BF)
    return pl.pallas_call(
        up_kernel,
        out_shape=[work, work, jax.ShapeDtypeStruct((64, HD), F32)],
        in_specs=[ANY, ANY, vmem, vmem],
        out_specs=[ANY, ANY, vmem],
        scratch_shapes=[
            pltpu.VMEM((8, UNIT, HD), BF),
            pltpu.VMEM((8, 2, 32, 512), BF),
            pltpu.VMEM((8, 2, 32, 512), BF),
            pltpu.VMEM((4, 2, 32, 1024), BF),
            pltpu.VMEM((2, 16, 1024), BF),
            pltpu.VMEM((2, 16, 1024), BF),
        ]
        + gather_sems("ctx", 1)
        + gather_sems("ctx", 1)
        + [dma((n,)) for n in (3, 4, 4, 4, 7, 8, 3, 4, 4, 2, 2)],
        compiler_params=pltpu.CompilerParams(
            collective_id=6, has_side_effects=True, vmem_limit_bytes=32 * 1024 * 1024
        ),
    )(image, text, w, up_w)


def silu(v):
    half = 0.5 * v
    return half + half * jnp.tanh(half)


def window_rows(latents):
    wide = jnp.pad(latents, ((0, 0), (0, 0), (8, 32)))
    before = wide[:, :, 0:512].reshape(2, 8, 16, 32)[..., :8]
    middle = latents.reshape(2, 8, 16, 32)
    after = wide[:, :, 40:552].reshape(2, 8, 16, 32)[..., :8]
    joined = jnp.concatenate([before, middle, after], axis=-1)
    return jnp.pad(joined, ((0, 0), (0, 0), (0, 0), (0, 80)))


def down_weights(down_all):
    down = jnp.concatenate([down_all[i, :72, :64] for i in range(4)], axis=1).reshape(3, 24, CH)
    return jnp.stack([jnp.pad(down, ((0, 0), (8 * c, 104 - 8 * c), (0, 0))) for c in range(4)]).reshape(4, 384, CH)


def tokens_kernel(g_ref, w_ref, patch_ref, out_ref, rows, total):
    px = pl.program_id(0)

    @pl.when(px == 0)
    def _():
        rows[...] = jnp.zeros_like(rows)
        for t in range(8):
            for s in range(2):
                for i in range(8):
                    r = 1 + 8 * t + i
                    rows[s, r // 4, r % 4] = g_ref[t, s, i]

    def window_row(k):
        return rows[:, pl.ds(k // 4, 16), k % 4].reshape(UNIT, HD)

    lhs = jnp.concatenate([window_row(px), window_row(px + 1), window_row(px + 2)], axis=1)
    acts = [silu(jnp.dot(lhs, w_ref[c], preferred_element_type=F32)).astype(BF) for c in range(4)]
    term = jnp.dot(jnp.concatenate(acts, axis=1), patch_ref[...], preferred_element_type=F32)

    @pl.when(px == 0)
    def _():
        total[...] = term

    @pl.when(px > 0)
    def _():
        total[...] += term

    @pl.when(px == 3)
    def _():
        out_ref[...] = total[...].astype(BF)


def tokens_of(latents_all, w, patch_in):
    return pl.pallas_call(
        tokens_kernel,
        grid=(4,),
        out_shape=jax.ShapeDtypeStruct((UNIT, HD), BF),
        in_specs=[
            pl.BlockSpec((8, 2, 8, 16, HD), lambda i: (0, 0, 0, 0, 0)),
            pl.BlockSpec((4, 384, CH), lambda i: (0, 0, 0)),
            pl.BlockSpec((4 * CH, HD), lambda i: (i, 0)),
        ],
        out_specs=pl.BlockSpec((UNIT, HD), lambda i: (0, 0)),
        scratch_shapes=[pltpu.VMEM((2, 17, 4, 16, HD), BF), pltpu.VMEM((UNIT, HD), F32)],
    )(latents_all, w, patch_in)


TILE = 256


def qkv_kernel(x_ref, gain_ref, wq_ref, wk_ref, wv_ref, qg_ref, kg_ref, q_ref, k_ref, v_ref):
    squares = jnp.zeros((TILE, HD), F32)
    for i in range(32):
        part = x_ref[i, 0].astype(F32)
        squares += part * part
    scale = lax.rsqrt(jnp.sum(squares, axis=1, keepdims=True) * (1.0 / 4096.0) + EPSILON)
    normed = jnp.concatenate(
        [
            (x_ref[i, 0].astype(F32) * scale * gain_ref[:, i * HD : (i + 1) * HD].astype(F32)).astype(BF)
            for i in range(32)
        ],
        axis=1,
    )

    def head(weight, gain, factor):
        raw = jnp.dot(normed, weight, preferred_element_type=F32)
        mean = jnp.mean(raw * raw, axis=1, keepdims=True)
        return (raw * lax.rsqrt(mean + EPSILON) * gain * factor).astype(BF)

    q_ref[...] = head(wq_ref[...], qg_ref[...], HD**-0.5)
    k_ref[...] = head(wk_ref[...], kg_ref[...], 1.0)
    v_ref[...] = jnp.dot(normed, wv_ref[...], preferred_element_type=F32).astype(BF)


def qkv_of(x, gain, wq, wk, wv, qg, kg):
    rows = pl.BlockSpec((TILE, HD), lambda i: (i, 0))
    weight = pl.BlockSpec((4096, HD), lambda i: (0, 0))
    small = pl.BlockSpec((1, HD), lambda i: (0, 0))
    return pl.pallas_call(
        qkv_kernel,
        grid=(UNIT // TILE,),
        out_shape=[jax.ShapeDtypeStruct((UNIT, HD), BF)] * 3,
        in_specs=[
            pl.BlockSpec((32, 1, TILE, HD), lambda i: (0, 0, i, 0)),
            pl.BlockSpec((1, 4096), lambda i: (0, 0)),
            weight,
            weight,
            weight,
            small,
            small,
        ],
        out_specs=[rows] * 3,
        compiler_params=pltpu.CompilerParams(vmem_limit_bytes=40 * 1024 * 1024),
    )(x, gain, wq, wk, wv, qg, kg)


def attention_kernel(top_ref, slot_ref, q_ref, lim_t_ref, lim_i_ref, text_ref, image_ref, out_ref):
    tile = pl.program_id(0)
    q = q_ref[...]
    cols = lax.broadcasted_iota(jnp.int32, (TILE, 1024), 1)

    def step(carry, k, v, limit):
        top, total, acc = carry
        s = lax.dot_general(q, k, (((1,), (1,)), ((), ())), preferred_element_type=F32)
        s = jnp.where(cols < limit, s, NEGATIVE)
        new = jnp.maximum(top, jnp.max(s, axis=1, keepdims=True))
        w = jnp.exp(s - new)
        factor = jnp.exp(top - new)
        total = total * factor + jnp.sum(w, axis=1, keepdims=True)
        acc = acc * factor + jnp.dot(w.astype(BF), v, preferred_element_type=F32)
        return new, total, acc

    def text_step(n, carry):
        k = jnp.concatenate([text_ref[2 * n, 0], text_ref[2 * n + 1, 0]], axis=0)
        v = jnp.concatenate([text_ref[2 * n, 1], text_ref[2 * n + 1, 1]], axis=0)
        return step(carry, k, v, lim_t_ref[...] - n * 1024)

    def image_step(n, carry):
        ks, vs = [], []
        for u in range(4):
            slot = slot_ref[n * 4 + u]
            rows = pl.ds(pl.multiple_of((slot % 2) * IMG_TOK, IMG_TOK), IMG_TOK)
            ks.append(image_ref[slot // 2, 0, rows])
            vs.append(image_ref[slot // 2, 1, rows])
        return step(carry, jnp.concatenate(ks, axis=0), jnp.concatenate(vs, axis=0), lim_i_ref[...] - n * 1024)

    carry = (jnp.full((TILE, 1), NEGATIVE, F32), jnp.zeros((TILE, 1), F32), jnp.zeros((TILE, HD), F32))
    carry = lax.fori_loop(0, (top_ref[1, tile] + 1023) // 1024, image_step, carry)
    carry = lax.fori_loop(0, (top_ref[0, tile] + 1023) // 1024, text_step, carry)
    _, total, acc = carry
    out_ref[...] = (acc / total).astype(BF)


def attention(slots, q, lim_t, lim_i, text, image):
    rows = q.shape[0]
    tops = jnp.stack([jnp.max(lim_t.reshape(-1, TILE), axis=1), jnp.max(lim_i.reshape(-1, TILE), axis=1)])
    whole = pl.BlockSpec((8, 2, UNIT, HD), lambda i, *_: (0, 0, 0, 0))
    grid_spec = pltpu.PrefetchScalarGridSpec(
        num_scalar_prefetch=2,
        grid=(rows // TILE,),
        in_specs=[
            pl.BlockSpec((TILE, HD), lambda i, *_: (i, 0)),
            pl.BlockSpec((TILE, 1), lambda i, *_: (i, 0)),
            pl.BlockSpec((TILE, 1), lambda i, *_: (i, 0)),
            whole,
            whole,
        ],
        out_specs=pl.BlockSpec((TILE, HD), lambda i, *_: (i, 0)),
    )
    return pl.pallas_call(
        attention_kernel,
        grid_spec=grid_spec,
        out_shape=jax.ShapeDtypeStruct((rows, HD), BF),
        compiler_params=pltpu.CompilerParams(vmem_limit_bytes=48 * 1024 * 1024),
    )(tops, slots, q, lim_t[:, None], lim_i[:, None], text, image)


def up_weights(up_conv):
    taps = up_conv.reshape(9, CH, CIN).transpose(1, 0, 2).reshape(CH, 72)
    row = lax.broadcasted_iota(jnp.int32, (72, 36 * HD), 0)
    col = lax.broadcasted_iota(jnp.int32, (72, 36 * HD), 1)
    cell, inner = col // HD, col % HD
    a, b = cell // 6 - inner // 32, cell % 6 - (inner // 8) % 4
    inside = (a >= 0) & (a <= 2) & (b >= 0) & (b <= 2)
    pick = jnp.where(inside & (row == (a * 3 + b) * 8 + inner % 8), 1.0, 0.0).astype(BF)
    return jnp.dot(taps, pick, preferred_element_type=F32).astype(BF)


def shards(
    text_embed,
    latents,
    down_conv,
    patch_in,
    norm_gain,
    query_weight,
    key_weight,
    value_weight,
    query_gain,
    key_gain,
    out_weight,
    patch_out,
    up_conv,
    span_start,
    image_of_slot,
):
    ctx = lax.axis_index("ctx")
    images = jnp.arange(16, dtype=jnp.int32)
    before = span_start - images * IMG_TOK
    is_slot = image_of_slot[None, :] == images[:, None]
    slot_of = jnp.sum(jnp.where(is_slot, images[None, :], 0), axis=1)

    latents_all, down_all = opening(window_rows(latents), jnp.pad(down_conv, ((0, 8), (0, 64))))
    image = tokens_of(latents_all, down_weights(down_all), patch_in)
    text_all, image_all, gains = gather_call(
        [("ctx", [text_embed]), ("xz", [image])], 3, gain=jnp.broadcast_to(norm_gain[None, :], (16, HD)), parts=2
    )
    image_all = image_all.reshape(32, 1, UNIT, HD)
    gain = gains[:, 0, :].reshape(1, 4096)

    text_rows = ctx * UNIT + jnp.arange(UNIT, dtype=jnp.int32)
    seen = jnp.sum((before[None, :] <= text_rows[:, None]).astype(jnp.int32), axis=1)
    text = jnp.take(text_all.reshape(8192, HD), text_rows + IMG_TOK * seen, axis=0, mode="clip")
    heads = (
        gain, query_weight, key_weight, value_weight, query_gain.reshape(1, HD), key_gain.reshape(1, HD)
    )
    image_q, image_k, image_v = qkv_of(image_all, *heads)
    image_kv, text_x = gather_call([("ctx", [image_k, image_v]), ("xz", [text])], 4, parts=2)
    text_x = text_x.reshape(32, 1, UNIT, HD)
    image_kv = image_kv.reshape(8, 2, UNIT, HD)
    text_q, text_k, text_v = qkv_of(text_x, *heads)
    text_kv, out_all, patch_all = gather_call(
        [("ctx", [text_k, text_v])], 5, weights=(out_weight.reshape(8, 4, HD, HD), patch_out), parts=2
    )
    text_kv = text_kv.reshape(8, 2, UNIT, HD)

    slots = ctx * 2 + jnp.arange(2, dtype=jnp.int32)
    here = slots[:, None] == images[None, :]
    own_image = jnp.sum(jnp.where(here, image_of_slot[None, :], 0), axis=1)
    own_before = jnp.sum(jnp.where(own_image[:, None] == images[None, :], before[None, :], 0), axis=1)
    spread = lambda pair: jnp.broadcast_to(pair[:, None], (2, IMG_TOK)).reshape(UNIT)
    image_mix = attention(
        slot_of, image_q, spread(own_before), spread((own_image + 1) * IMG_TOK), text_kv, image_kv
    )
    text_mix = attention(slot_of, text_q, text_rows + 1, seen * IMG_TOK, text_kv, image_kv)

    image_out, text_out = mix(image_mix, text_mix, out_all.reshape(4, 1024, HD), image, text)
    image_work, text_work, cells = up_block(image_out, text_out, patch_all, up_weights(up_conv))
    noise_pred = cells.reshape(2, 2, 16, 4, 32).transpose(0, 1, 3, 2, 4).reshape(2, 8, 512)

    positions = ctx * 1024 + jnp.arange(1024, dtype=jnp.int32)
    started = (span_start[None, :] <= positions[:, None]).astype(jnp.int32)
    passed = jnp.sum((span_start[None, :] + IMG_TOK <= positions[:, None]).astype(jnp.int32), axis=1)
    inside = jnp.sum(started, axis=1) > passed
    now = passed[:, None] == images[None, :]
    slot = jnp.sum(jnp.where(now, slot_of[None, :], 0), axis=1)
    start = jnp.sum(jnp.where(now, span_start[None, :], 0), axis=1)
    row = positions - passed * IMG_TOK
    text_part = jnp.take(text_work.reshape(4096, HD), row, axis=0, mode="clip")
    image_part = jnp.take(
        image_work.reshape(4096, HD), slot * IMG_TOK + positions - start, axis=0, mode="clip"
    )
    layer_out = jnp.where(inside[:, None], image_part, text_part)
    return layer_out, noise_pred


def solution(mesh):
    return jax.shard_map(
        shards,
        mesh=mesh,
        in_specs=(
            P("ctx", ("tile", "mp")),
            P("ctx", "tile", None),
            P(None, "mp"),
            P(None, ("tile", "mp")),
            P(("tile", "mp")),
            P(None, ("tile", "mp")),
            P(None, ("tile", "mp")),
            P(None, ("tile", "mp")),
            P(),
            P(),
            P(None, ("tile", "mp")),
            P(("tile", "mp"), None),
            P(),
            P(),
            P(),
        ),
        out_specs=(P("ctx", ("tile", "mp")), P("ctx", "tile", None)),
        check_vma=False,
    )
```

time: 383 us -> 320 us (0.84)
  Pallas kernels: 324 us -> 282 us
  local copies, waits for them, and re-layouts: 51 us -> 29.2 us
    pallas_call x11 -> x9, Pallas kernels: 313 us -> 268 us  [the longest x3 143 us: gather_call(): pl.pallas_call(kernel, out_shape=shapes, in_specs=[ANY] * len(inputs_in),...]
    slice x19 -> x2, local copies, waits for them, and re-layouts: 22.5 us -> 1.66 us  [the longest x1 0.87 us: window_rows(): before = wide[:, :, 0:512].reshape(2, 8, 16, 32)[..., :8]]
    pallas_call x1 -> x2, Pallas kernels: 11 us -> 13.9 us  [attention(): pl.pallas_call(attention_kernel, grid_spec=grid_spec, out_shape=jax.Shape...]
    unnamed x45 -> x59, local copies, waits for them, and re-layouts: 12.8 us -> 13.5 us
where the time goes in v2:
time: 320 us; the launch traced here: 319 us
  Pallas kernels  282 us (88%)
  local copies, waits for them, and re-layouts  29.2 us (9%)
  other arithmetic  4.98 us (2%)
    pallas_call x3, Pallas kernels, gather_call(): pl.pallas_call(kernel, out_shape=shapes, in_specs=[ANY] * len(inputs_in),...  143 us
    pallas_call x1, Pallas kernels, up_block(): pl.pallas_call(up_kernel, out_shape=[work, work, jax.ShapeDtypeStruct((64...  54 us
    pallas_call x1, Pallas kernels, mix(): pl.pallas_call(mix_kernel, out_shape=[jax.ShapeDtypeStruct((UNIT, HD), BF...  36.5 us
    pallas_call x1, Pallas kernels, opening(): pl.pallas_call(opening_kernel, out_shape=[jax.ShapeDtypeStruct((8,) + lat...  17.7 us
    pallas_call x2, Pallas kernels, attention(): pl.pallas_call(attention_kernel, grid_spec=grid_spec, out_shape=jax.Shape...  13.9 us
    unnamed x59, local copies, waits for them, and re-layouts  13.5 us
    pallas_call x2, Pallas kernels, qkv_of(): pl.pallas_call(qkv_kernel, grid=(UNIT // TILE,), out_shape=[jax.ShapeDtyp...  10.1 us
    pallas_call x1, Pallas kernels, tokens_of(): pl.pallas_call(tokens_kernel, grid=(4,), out_shape=jax.ShapeDtypeStruct((...  6.59 us

profile of v2, /device:TPU:1, one launch (start us, length us, event | category | flops | bytes accessed | tf_op | source)
XLA Modules:
  0.0 319.0 jit_solution(16431555867531847113)
XLA Ops:
  0.6 0.9 pad_slice_fusion.1
  4.7 17.7 %shard_map.158 = (bf16[8,2,8,16,128]{4,3,2,1,0:T(8,128)(2,1)}, bf16[4,80,128]{2,1,0:T(8,128)(2,1)}) custom-call(bf16[2,8,16,128]{3,2,1,0:T(8,128)(2,1)} %fusion.44.latents, bf16[80,128]{1,0:T(8,128)(2,1)} %pad.30.down), custom_call_target="tpu_custom_call" | custom-call | tf_op jit(solution)/shard_map/pallas_call | solution.py:408
  23.4 1.0 pad_maximum_fusion.w_ref
  24.4 6.6 %shard_map.159.refs_1_.image_stream = bf16[512,128]{1,0:T(8,128)(2,1)} custom-call(bf16[8,2,8,16,128]{4,3,2,1,0:T(8,128)(2,1)} %get-tuple-element.23.g_ref, bf16[4,384,256]{2,1,0:T(8,128)(2,1)} %pad_maximum_fusion.w_ref, bf16[4096,128]{1,0:T(8,128)(2,1)} %patch_ref.1), custom_call_target="tpu_custom_call" | custom-call | tf_op jit(solution)/shard_map/pallas_call | solution.py:713
  31.6 58.1 %shard_map.160 = (bf16[8,2,512,128]{3,2,1,0:T(8,128)(2,1)}, bf16[32,2,256,128]{3,2,1,0:T(8,128)(2,1)}, bf16[32,16,128]{2,1,0:T(8,128)(2,1)}) custom-call(bf16[1024,128]{1,0:T(8,128)(2,1)} %refs_0_.1, bf16[512,128]{1,0:T(8,128)(2,1)} %shard_map.159.refs_1_.image_stream, bf16[16,128]{1,0:T(8,128)(2,1)} %broadcast_in_dim.115.refs_2_), custom_call_target="tpu_custom_call" | custom-call | tf_op jit(solution)/shard_map/pallas_call | solution.py:368
  89.7 0.9 slice_bitcast_fusion.gain_ref
  90.6 2.2 copy-done.4
  92.8 5.0 %shard_map.161 = (bf16[512,128]{1,0:T(8,128)(2,1)S(1)}, bf16[512,128]{1,0:T(8,128)(2,1)S(1)}, bf16[512,128]{1,0:T(8,128)(2,1)S(1)}) custom-call(bf16[32,1,512,128]{3,2,1,0:T(8,128)(2,1)S(1)} %bitcast.61, bf16[1,4096]{1,0:T(2,128)(2,1)S(1)} %slice_bitcast_fusion.gain_ref, bf16[4096,128]{1,0:T(8,128)(2,1)S(1)} %copy-done.6, bf16[4096,128]{1,0:T(8,128)(2,1)S(1)} %copy-done.7, ...), custom_call_target="tpu_custom_call" | custom-call | tf_op jit(solution)/shard_map/pallas_call | solution.py:758
  100.7 3.5 %gather_fusion = bf16[512,128]{1,0:T(8,128)(2,1)} fusion(bf16[8192,128]{1,0:T(8,128)(2,1)} %bitcast.75, s32[1024]{0:T(1024)S(1)} %pad_clamp_fusion), kind=kCustom, calls=%fused_computation | custom fusion | bytes 264192 | tf_op jit(solution)/shard_map/jit(_take)/gather | solution.py:881
  104.3 43.6 %shard_map.162 = (bf16[8,4,256,128]{3,2,1,0:T(8,128)(2,1)}, bf16[32,2,256,128]{3,2,1,0:T(8,128)(2,1)}) custom-call(bf16[512,128]{1,0:T(8,128)(2,1)} %copy-done.16, bf16[512,128]{1,0:T(8,128)(2,1)} %copy-done.17, bf16[512,128]{1,0:T(8,128)(2,1)} %gather_fusion), custom_call_target="tpu_custom_call" | custom-call | tf_op jit(solution)/shard_map/pallas_call | solution.py:368
  147.8 2.2 copy-done.5
  150.0 5.1 %shard_map.163 = (bf16[512,128]{1,0:T(8,128)(2,1)S(1)}, bf16[512,128]{1,0:T(8,128)(2,1)S(1)}, bf16[512,128]{1,0:T(8,128)(2,1)S(1)}) custom-call(bf16[32,1,512,128]{3,2,1,0:T(8,128)(2,1)S(1)} %bitcast.62, bf16[1,4096]{1,0:T(2,128)(2,1)S(1)} %slice_bitcast_fusion.gain_ref, bf16[4096,128]{1,0:T(8,128)(2,1)S(1)} %copy-done.6, bf16[4096,128]{1,0:T(8,128)(2,1)S(1)} %copy-done.7, ...), custom_call_target="tpu_custom_call" | custom-call | tf_op jit(solution)/shard_map/pallas_call | solution.py:758
  157.1 41.7 %shard_map.164 = (bf16[8,4,256,128]{3,2,1,0:T(8,128)(2,1)}, bf16[4,8,128,128]{3,2,1,0:T(8,128)(2,1)}, bf16[8,128,512]{2,1,0:T(8,128)(2,1)}) custom-call(bf16[512,128]{1,0:T(8,128)(2,1)} %copy-done.20, bf16[512,128]{1,0:T(8,128)(2,1)} %copy-done.21, bf16[8,4,128,128]{3,2,1,0:T(8,128)(2,1)} %bitcast.70, bf16[128,4096]{1,0:T(8,128)(2,1)} %refs_3_.1), custom_call_target="tpu_custom_call" | custom-call | tf_op jit(solution)/shard_map/pallas_call | solution.py:368
  199.2 1.6 copy-done.2
  200.8 0.9 copy-done.19
  201.7 4.1 %shard_map.166.text = bf16[512,128]{1,0:T(8,128)(2,1)S(1)} custom-call(s32[2,2]{1,0:T(2,128)S(1)} %pad_add_fusion.1.top_ref, s32[16]{0:T(128)S(1)} %select_reduce_fusion.2.slot_ref, bf16[512,128]{1,0:T(8,128)(2,1)S(1)} %copy-done.19, s32[512,1]{1,0:T(8,128)S(1)} %copy-done.12, s32[512,1]{1,0:T(8,128)S(1)} %copy.28.lim_i_ref, ...), custom_call_target="tpu_custom_call" | custom-call | tf_op jit(solution)/shard_map/pallas_call | solution.py:829
  207.0 1.6 copy-done.3
  208.6 9.8 %shard_map.165.image = bf16[512,128]{1,0:T(8,128)(2,1)S(1)} custom-call(s32[2,2]{1,0:T(2,128)S(1)} %pad_add_fusion.top_ref, s32[16]{0:T(128)S(1)} %select_reduce_fusion.2.slot_ref, bf16[512,128]{1,0:T(8,128)(2,1)S(1)} %copy-done.15, s32[512,1]{1,0:T(8,128)S(1)} %bitcast.63, s32[512,1]{1,0:T(8,128)S(1)} %bitcast.64, bf16[8,2,512,128]{3,2,1,0:T(8,128)(2,1)S(1)} %bitcast.58, ...), custom_call_target="tpu_custom_call" | custom-call | tf_op jit(solution)/shard_map/pallas_call | solution.py:829
  218.4 36.5 %shard_map.167 = (bf16[512,128]{1,0:T(8,128)(2,1)S(1)}, bf16[512,128]{1,0:T(8,128)(2,1)S(1)}) custom-call(bf16[512,128]{1,0:T(8,128)(2,1)S(1)} %shard_map.165.image, bf16[512,128]{1,0:T(8,128)(2,1)S(1)} %shard_map.166.text, bf16[4,1024,128]{2,1,0:T(8,128)(2,1)S(1)} %bitcast.65, bf16[512,128]{1,0:T(8,128)(2,1)S(1)} %copy-done.9, bf16[512,128]{1,0:T(8,128)(2,1)S(1)} %copy-done.10), custom_call_target="tpu_custom_call" | custom-call | tf_op jit(solution)/shard_map/pallas_call | solution.py:466
  255.0 1.5 fusion.up_ref
  256.5 54.0 %shard_map.168 = (bf16[8,1,512,128]{3,2,1,0:T(8,128)(2,1)S(1)}, bf16[8,1,512,128]{3,2,1,0:T(8,128)(2,1)S(1)}, f32[64,128]{1,0:T(8,128)S(1)}) custom-call(bf16[512,128]{1,0:T(8,128)(2,1)S(1)} %get-tuple-element.38.image, bf16[512,128]{1,0:T(8,128)(2,1)S(1)} %get-tuple-element.39.text, bf16[8,128,512]{2,1,0:T(8,128)(2,1)S(1)} %copy-done.11, ...), custom_call_target="tpu_custom_call" | custom-call | tf_op jit(solution)/shard_map/pallas_call | solution.py:639
  310.7 3.2 %gather_fusion.2 = bf16[1024,128]{1,0:T(8,128)(2,1)S(1)} fusion(bf16[4096,128]{1,0:T(8,128)(2,1)S(1)} %bitcast.60, s32[1024]{0:T(1024)S(1)} %broadcast_clamp_fusion), kind=kCustom, calls=%fused_computation.2 | custom fusion | bytes 528384 | tf_op jit(solution)/shard_map/jit(_take)/gather | solution.py:917
  314.0 3.2 %gather_fusion.1 = bf16[1024,128]{1,0:T(8,128)(2,1)S(1)} fusion(bf16[4096,128]{1,0:T(8,128)(2,1)S(1)} %bitcast.59, s32[1024]{0:T(1024)S(1)} %broadcast_clamp_fusion.1), kind=kCustom, calls=%fused_computation.1 | custom fusion | bytes 528384 | tf_op jit(solution)/shard_map/jit(_take)/gather | solution.py:918
  317.2 0.9 broadcast_select_fusion
  (97 shorter events, 12.2 us)
Async XLA Ops:
  0.6 254.3 %copy-start = (bf16[2304,8]{0,1:T(8,128)(2,1)S(1)}, bf16[2304,8]{0,1:T(8,128)(2,1)}, u32[]{:S(2)}) copy-start(bf16[2304,8]{0,1:T(8,128)(2,1)} %param.27) | copy-start | bytes 110596
  23.4 67.1 %copy-start.8 = (bf16[4096,128]{1,0:T(8,128)(2,1)S(1)}, bf16[4096,128]{1,0:T(8,128)(2,1)}, u32[]{:S(2)}) copy-start(bf16[4096,128]{1,0:T(8,128)(2,1)} %wv_ref.3) | copy-start | bytes 3145732
  24.4 6.6 %copy-start.25 = (bf16[128]{0:T(256)(128)(2,1)S(1)}, bf16[128]{0:T(256)(128)(2,1)}, u32[]{:S(2)}) copy-start(bf16[128]{0:T(256)(128)(2,1)} %param.19) | copy-start | bytes 772
  24.4 66.1 %copy-start.6 = (bf16[4096,128]{1,0:T(8,128)(2,1)S(1)}, bf16[4096,128]{1,0:T(8,128)(2,1)}, u32[]{:S(2)}) copy-start(bf16[4096,128]{1,0:T(8,128)(2,1)} %wq_ref.3) | copy-start | bytes 3145732
  24.4 66.1 %copy-start.7 = (bf16[4096,128]{1,0:T(8,128)(2,1)S(1)}, bf16[4096,128]{1,0:T(8,128)(2,1)}, u32[]{:S(2)}) copy-start(bf16[4096,128]{1,0:T(8,128)(2,1)} %wk_ref.3) | copy-start | bytes 3145732
  24.4 66.2 %copy-start.22 = (f32[128]{0:T(128)S(1)}, f32[128]{0:T(128)}, u32[]{:S(2)}) copy-start(f32[128]{0:T(128)} %param.23) | copy-start | bytes 1540
  24.4 66.2 %copy-start.23 = (f32[128]{0:T(128)S(1)}, f32[128]{0:T(128)}, u32[]{:S(2)}) copy-start(f32[128]{0:T(128)} %param.24) | copy-start | bytes 1540
  90.6 2.2 copy-start.4
  92.8 6.9 %copy-start.24 = (s32[16]{0:T(128)S(1)}, s32[16]{0:T(128)}, u32[]{:S(2)}) copy-start(s32[16]{0:T(128)} %param.28) | copy-start | bytes 196
  99.1 0.7 copy-start.17
  147.8 2.2 copy-start.5
  155.8 0.7 copy-start.20
  156.5 0.6 copy-start.21
  157.1 42.0 %copy-start.26 = (s32[16]{0:T(128)S(1)}, s32[16]{0:T(128)}, u32[]{:S(2)}) copy-start(s32[16]{0:T(128)} %param.29) | copy-start | bytes 196
  157.1 42.1 %copy-start.1 = (bf16[8,4,256,128]{3,2,1,0:T(8,128)(2,1)S(1)}, bf16[8,4,256,128]{3,2,1,0:T(8,128)(2,1)}, u32[]{:S(2)}) copy-start(bf16[8,4,256,128]{3,2,1,0:T(8,128)(2,1)} %get-tuple-element.35) | copy-start | bytes 6291460
  157.1 42.1 %copy-start.12 = (s32[512,1]{1,0:T(8,128)S(1)}, s32[512,1]{1,0:T(8,128)}, u32[]{:S(2)}) copy-start(s32[512,1]{1,0:T(8,128)} %get-tuple-element.65.lim_t_ref) | copy-start | bytes 6148
  199.2 1.6 copy-start.2
  200.8 0.9 copy-start.19
  201.7 5.2 %copy-start.15 = (bf16[512,128]{1,0:T(8,128)(2,1)S(1)}, bf16[512,128]{1,0:T(8,128)(2,1)}, u32[]{:S(2)}) copy-start(bf16[512,128]{1,0:T(8,128)(2,1)} %copy-done.14) | copy-start | bytes 393220
  207.0 1.6 copy-start.3
  208.6 9.8 %copy-start.9 = (bf16[512,128]{1,0:T(8,128)(2,1)S(1)}, bf16[512,128]{1,0:T(8,128)(2,1)}, u32[]{:S(2)}) copy-start(bf16[512,128]{1,0:T(8,128)(2,1)} %shard_map.159.refs_1_.image_stream) | copy-start | bytes 393220
  208.6 9.8 %copy-start.10 = (bf16[512,128]{1,0:T(8,128)(2,1)S(1)}, bf16[512,128]{1,0:T(8,128)(2,1)}, u32[]{:S(2)}) copy-start(bf16[512,128]{1,0:T(8,128)(2,1)} %gather_fusion) | copy-start | bytes 393220
  208.6 9.8 %copy-start.13 = (bf16[4,8,128,128]{3,2,1,0:T(8,128)(2,1)S(1)}, bf16[4,8,128,128]{3,2,1,0:T(8,128)(2,1)}, u32[]{:S(2)}) copy-start(bf16[4,8,128,128]{3,2,1,0:T(8,128)(2,1)} %get-tuple-element.37) | copy-start | bytes 3145732
  255.0 1.5 copy-start.11
  (3 other events, 1.9 us)

commit v3 on v2

v3 whole, which is shorter than its diff:
```python
import functools

import jax
import jax.numpy as jnp
from jax import lax
from jax.experimental import pallas as pl
from jax.experimental.pallas import tpu as pltpu
from jax.sharding import PartitionSpec as P

HD = 128
CH = 256
CIN = 8
PATCH = 4
IMG_TOK = 256
UNIT = 512
EPSILON = 1e-05
NEGATIVE = -1e30
MESH = pl.DeviceIdType.MESH
ANY = pl.BlockSpec(memory_space=pl.ANY)
BF = jnp.bfloat16
F32 = jnp.float32


def remote(src, dst, send, recv, device):
    return pltpu.make_async_remote_copy(
        src_ref=src, dst_ref=dst, send_sem=send, recv_sem=recv, device_id=device, device_id_type=MESH
    )


def barrier(devices):
    sem = pltpu.get_barrier_semaphore()
    for device in devices:
        pl.semaphore_signal(sem, inc=1, device_id=device, device_id_type=MESH)
    pl.semaphore_wait(sem, len(devices))


def coordinates():
    return lax.axis_index("ctx"), lax.axis_index("tile"), lax.axis_index("mp")


LAG = 1.0


class Gather:
    def __init__(self, over, sources, dst, send, recv, local):
        ctx, tile, mp = coordinates()
        self.dst, self.send, self.recv, self.local = dst, send, recv, local
        self.rows = dst.shape[2]
        parts = dst.shape[1] // len(sources)
        self.sources = [
            source.at[pl.ds(part * self.rows, self.rows)] for source in sources for part in range(parts)
        ]
        self.pending, self.count = [], 0
        if over != "ctx":
            a = tile // 2
            self.a, self.r, self.core = a, mp, tile % 2
            self.dev = lambda a, r, core: (ctx, a * 2 + core, r)
            if over == "xz":
                self.slot = lambda a, r, core: (a * 2 + core) * 4 + r
            else:
                self.slot = lambda a, r, core: a * 2 + core
            self.sibling = 1 - self.core
            near = a + 1 - 2 * (a % 2)
            cross = 2 - a // 2
            self.order = [a, near, cross, 3 * (1 - a // 2)]
            self.onward = [None, 3 - a, near, near]
            self.middle = (a == 1) | (a == 2)
            self.inner, self.outer = 1 + a % 2, near
            self.others = [(a + d) % 4 for d in range(1, 4)]
        else:
            a = ctx // 4
            self.a, self.r, self.core = a, ctx % 4, 0
            self.dev = lambda a, r, core: (a * 4 + r, tile, mp)
            self.slot = lambda a, r, core: a * 4 + r
            self.sibling = None
            self.order = [a, 1 - a]
            self.middle = None
            self.inner = 1 - a
            self.others = [1 - a]
        self.right, self.left, self.far = (self.r + 1) % 4, (self.r + 3) % 4, (self.r + 2) % 4

    def partners(self):
        found = [self.dev(a, self.r, self.core) for a in self.others]
        found += [self.dev(self.a, self.right, self.core), self.dev(self.a, self.left, self.core)]
        if self.sibling is not None:
            found.append(self.dev(self.a, self.r, self.sibling))
        return found

    def push(self, src, slot, unit, device, half=None, when=None):
        dst = self.dst.at[slot, unit]
        which = 0
        if half is not None:
            rows = pl.ds(half * (self.rows // 2), self.rows // 2)
            src, dst, which = src.at[rows], dst.at[rows], half
        count = self.count
        self.count += 1
        make = lambda: remote(src, dst, self.send.at[count], self.recv.at[unit, slot, which], device)
        self.pending.append((make, when))
        if when is None:
            make().start()
        else:
            pl.when(when)(lambda: make().start())

    def arrive(self, slot, unit, half=None):
        dst = self.dst.at[slot, unit]
        which = 0
        if half is not None:
            dst, which = dst.at[pl.ds(half * (self.rows // 2), self.rows // 2)], half
        device = self.dev(self.a, self.right, self.core)
        remote(dst, dst, self.send.at[0], self.recv.at[unit, slot, which], device).wait_recv()

    def forward(self, k, unit):
        slot = self.slot(self.order[k], self.r, self.core)
        self.arrive(slot, unit)
        src = self.dst.at[slot, unit]
        if self.middle is not None:
            self.push(src, slot, unit, self.dev(self.onward[k], self.r, self.core), when=self.middle)
        self.push(src, slot, unit, self.dev(self.a, self.right, self.core))
        self.push(src, slot, unit, self.dev(self.a, self.left, self.core))
        self.twin(slot, unit)

    def twin(self, slot, unit):
        if self.sibling is not None:
            src = self.dst.at[slot, unit]
            self.push(src, slot, unit, self.dev(self.a, self.r, self.sibling))

    def halves(self, k, unit):
        for ring, target, half in ((self.left, self.right, 0), (self.right, self.left, 1)):
            slot = self.slot(self.order[k], ring, self.core)
            self.arrive(slot, unit)
            self.push(self.dst.at[slot, unit], slot, unit, self.dev(self.a, target, self.core), half)
            self.twin(slot, unit)

    def ends(self, k, unit):
        slot = self.slot(self.order[k], self.far, self.core)
        self.arrive(slot, unit, 0)
        self.arrive(slot, unit, 1)
        self.twin(slot, unit)

    def events(self, start=0.0):
        units = len(self.sources)
        self.own_copies = []

        def begin():
            own = self.slot(self.a, self.r, self.core)
            for u, src in enumerate(self.sources):
                self.push(src, own, u, self.dev(self.inner, self.r, self.core))
                if self.middle is not None:
                    self.push(src, own, u, self.dev(self.outer, self.r, self.core), when=self.middle)
                self.push(src, own, u, self.dev(self.a, self.right, self.core))
                self.push(src, own, u, self.dev(self.a, self.left, self.core))
                if self.sibling is not None:
                    self.push(src, own, u, self.dev(self.a, self.r, self.sibling))
            for u, src in enumerate(self.sources):
                copy = pltpu.make_async_copy(src, self.dst.at[own, u], self.local.at[u])
                copy.start()
                self.own_copies.append(copy)

        found = [(0.0, begin)]
        step = 4.0 / units
        for k in range(len(self.order)):
            for u in range(units):
                at = (k * units + u) * step
                if k > 0:
                    found.append((at, lambda k=k, u=u: self.forward(k, u)))
                found.append((at + LAG * 4.0 + 0.3, lambda k=k, u=u: self.halves(k, u)))
                found.append((at + LAG * 8.0 + 0.6, lambda k=k, u=u: self.ends(k, u)))
        found.append((25.0 if self.sibling is not None else 14.0, self.complete))
        found.append((2000.0, self.close))
        return [(start + at, act) for at, act in found]

    def complete(self):
        if self.sibling is not None:
            for a in self.order:
                for ring in (self.r, self.left, self.right, self.far):
                    for u in range(len(self.sources)):
                        self.arrive(self.slot(a, ring, self.sibling), u)
        for copy in self.own_copies:
            copy.wait()

    def close(self):
        for make, when in self.pending:
            if when is None:
                make().wait_send()
            else:
                pl.when(when)(lambda make=make: make().wait_send())

    def column_events(self, done):
        units = len(self.sources)
        link = 2 * self.rows * 2 * HD / 92000
        hop = 2.0
        own = self.slot(self.a, self.r, self.core)
        twin = self.dev(self.a, self.r, self.sibling)
        self.own_copies = []

        def begin(u):
            src = self.sources[u]
            self.push(src, own, u, self.dev(self.inner, self.r, self.core))
            self.push(src, own, u, self.dev(self.outer, self.r, self.core), when=self.middle)
            self.push(src, own, u, twin)
            copy = pltpu.make_async_copy(src, self.dst.at[own, u], self.local.at[u])
            copy.start()
            self.own_copies.append(copy)

        def pass_on(k, u):
            slot = self.slot(self.order[k], self.r, self.core)
            self.arrive(slot, u)
            src = self.dst.at[slot, u]
            self.push(src, slot, u, self.dev(self.onward[k], self.r, self.core), when=self.middle)
            self.push(src, slot, u, twin)

        def whole(u):
            self.own_copies[u].wait()
            for k in range(4):
                self.arrive(self.slot(self.order[k], self.r, self.sibling), u)
            done(u)

        found = []
        for u in range(units):
            at = u * 3 * link
            found.append((max(at - 2 * hop, 0.0), lambda u=u: begin(u)))
            for k in range(1, 4):
                found.append((at + k * (link + hop), lambda k=k, u=u: pass_on(k, u)))
            found.append((at + 3 * (link + hop) + hop, lambda u=u: whole(u)))
        return found

    def close_column(self):
        for make, when in self.pending:
            if when is None:
                make().wait_send()
            else:
                pl.when(when)(lambda make=make: make().wait_send())


def perform(events):
    for _, act in sorted(events, key=lambda event: event[0]):
        act()


def gather_sems(over, units):
    slots, sends = {"xz": (32, 37), "ctx": (8, 9), "z": (8, 9)}[over]
    return [
        pltpu.SemaphoreType.DMA((units * sends,)),
        pltpu.SemaphoreType.DMA((units, slots, 2)),
        pltpu.SemaphoreType.DMA((units,)),
    ]


class Weights:
    def __init__(self, out_weight, patch_out, out_all, patch_all, out_send, out_recv, patch_send, patch_recv, local):
        self.ctx, self.tile, self.mp = coordinates()
        self.core, self.z = self.tile % 2, self.tile // 2
        self.out_weight, self.patch_out, self.out_all, self.patch_all = out_weight, patch_out, out_all, patch_all
        self.out_send, self.out_recv, self.patch_send, self.patch_recv = out_send, out_recv, patch_send, patch_recv
        self.local = local

    def mates(self):
        found = []
        for i in range(1, 8):
            core, mp = (self.core + i // 4) % 2, (self.mp + i) % 4
            found.append((core, mp, (self.ctx, self.z * 2 + core, mp)))
        return found

    def partners(self):
        return [device for _, _, device in self.mates()]

    def columns(self, core, mp):
        return self.patch_out.at[:, pl.ds(pl.multiple_of(mp * 1024 + core * 512, 512), 512)]

    def events(self, start=0.0):
        own = self.core * 4 + self.mp
        copies = []
        for i, (core, mp, device) in enumerate(self.mates()):
            if i < 3:
                copies.append(
                    remote(
                        self.out_weight.at[:, mp], self.out_all.at[self.mp], self.out_send.at[i],
                        self.out_recv.at[self.mp], device,
                    )
                )
            copies.append(
                remote(
                    self.columns(core, mp), self.patch_all.at[own], self.patch_send.at[i],
                    self.patch_recv.at[own], device,
                )
            )
        here = [
            pltpu.make_async_copy(self.out_weight.at[:, self.mp], self.out_all.at[self.mp], self.local.at[0]),
            pltpu.make_async_copy(self.columns(self.core, self.mp), self.patch_all.at[own], self.local.at[1]),
        ]

        def begin():
            for copy in copies + here:
                copy.start()

        def end():
            for i, (core, mp, device) in enumerate(self.mates()):
                slot = core * 4 + mp
                if i < 3:
                    dst = self.out_all.at[mp]
                    remote(dst, dst, self.out_send.at[0], self.out_recv.at[mp], device).wait_recv()
                dst = self.patch_all.at[slot]
                remote(dst, dst, self.patch_send.at[0], self.patch_recv.at[slot], device).wait_recv()
            for copy in copies:
                copy.wait_send()
            for copy in here:
                copy.wait()

        return [(start, begin), (1000.0, end)]


def weight_sems():
    return [pltpu.SemaphoreType.DMA((n,)) for n in (3, 4, 7, 8, 2)]


def merge(groups):
    return [device for group in groups for device in group]


def silu(v):
    half = 0.5 * v
    return half + half * jnp.tanh(half)


def opening_kernel(
    pairs, down, text, patch_ref, gain_ref, image_ref, text_all,
    pairs_all, down_all, rows, weights, total,
    pair_send, pair_recv, down_send, down_recv, own_sem, send, recv, local,
):
    ctx, tile, mp = coordinates()
    job = Gather("ctx", [text], text_all, send, recv, local)
    tiles = [((tile + i) % 8) for i in range(1, 8)]
    mps = [((mp + i) % 4) for i in range(1, 4)]
    barrier([(ctx, t, mp) for t in tiles] + [(ctx, tile, m) for m in mps] + job.partners())
    copies = []
    for i, t in enumerate(tiles):
        copies.append(remote(pairs, pairs_all.at[tile], pair_send.at[i], pair_recv.at[tile], (ctx, t, mp)))
    for i, m in enumerate(mps):
        copies.append(remote(down, down_all.at[mp], down_send.at[i], down_recv.at[mp], (ctx, tile, m)))
    own = [
        pltpu.make_async_copy(pairs, pairs_all.at[tile], own_sem.at[0]),
        pltpu.make_async_copy(down, down_all.at[mp], own_sem.at[1]),
    ]
    for copy in copies + own:
        copy.start()

    def prepare():
        rows[...] = jnp.zeros_like(rows)
        weights[...] = jnp.zeros_like(weights)

    def arrange():
        for copy in own:
            copy.wait()
        for m in mps:
            remote(down, down_all.at[m], down_send.at[0], down_recv.at[m], (ctx, tile, m)).wait_recv()
        taps = sum(down_all[m].astype(F32) for m in range(4))
        for kind in range(2):
            for a in range(3):
                at = (a + 1 - kind) // 2 * HD + (a + 1 - kind) % 2 * 48
                for pc in range(4):
                    weights[kind * 4 + pc, at + 8 * pc : at + 8 * pc + 24] = taps[24 * a : 24 * a + 24]
        for t in tiles:
            remote(pairs, pairs_all.at[t], pair_send.at[0], pair_recv.at[t], (ctx, t, mp)).wait_recv()
        for t in range(8):
            for s in range(2):
                for i in range(4):
                    at = 1 + 4 * t + i
                    rows[s, at // 2, at % 2] = pairs_all[t, s, i]

    def pixel_row(pr):
        first = (0, 1, 1, 2)[pr]
        lhs = jnp.concatenate(
            [rows[:, p // 2 : p // 2 + 16, p % 2].reshape(UNIT, HD) for p in (first, first + 1)], axis=1
        )
        acts = [
            silu(jnp.dot(lhs, weights[pr % 2 * 4 + pc].astype(BF), preferred_element_type=F32)).astype(BF)
            for pc in range(4)
        ]
        term = jnp.dot(
            jnp.concatenate(acts, axis=1), patch_ref[pr * 1024 : (pr + 1) * 1024], preferred_element_type=F32
        )
        if pr == 0:
            total[...] = term
        elif pr < 3:
            total[...] += term
        else:
            image_ref[:UNIT] = (total[...] + term).astype(BF)
            image_ref[UNIT:] = jnp.broadcast_to(gain_ref[...], (32, HD))

    perform(
        job.events()
        + [(0.1, prepare), (1.0, arrange)]
        + [(at, lambda pr=pr: pixel_row(pr)) for pr, at in enumerate((1.5, 4.4, 7.0, 9.0))]
    )
    for copy in copies:
        copy.wait_send()


def opening(pairs, down, text, patch_in, gain, parts=2):
    dma = pltpu.SemaphoreType.DMA
    vmem = pl.BlockSpec(memory_space=pltpu.VMEM)
    return pl.pallas_call(
        opening_kernel,
        out_shape=[
            jax.ShapeDtypeStruct((UNIT + 32, HD), BF),
            jax.ShapeDtypeStruct((8, parts, 1024 // parts, HD), BF),
        ],
        in_specs=[ANY, ANY, ANY, vmem, vmem],
        out_specs=[vmem, ANY],
        scratch_shapes=[
            pltpu.VMEM((8,) + pairs.shape, BF),
            pltpu.VMEM((4,) + down.shape, BF),
            pltpu.VMEM((2, 17, 2, 16, HD), BF),
            pltpu.VMEM((8, 2 * HD, CH), F32),
            pltpu.VMEM((UNIT, HD), F32),
        ]
        + [dma((7,)), dma((8,)), dma((3,)), dma((4,)), dma((2,))]
        + gather_sems("ctx", parts),
        compiler_params=pltpu.CompilerParams(
            collective_id=1, has_side_effects=True, vmem_limit_bytes=32 * 1024 * 1024
        ),
    )(pairs, down, text, patch_in, gain)


TILE = 256


def heads_kernel(
    image, text, wq_ref, wk_ref, wv_ref, qg_ref, kg_ref, out_weight, patch_out,
    image_q, text_q, image_kv, text_kv, out_all, patch_all,
    image_x, text_x, image_own, text_own, *sems
):
    image_job = Gather("xz", [image], image_x, *sems[0:3])
    text_job = Gather("xz", [text], text_x, *sems[3:6])
    image_keys = Gather("ctx", [image_own.at[0], image_own.at[1]], image_kv, *sems[6:9])
    text_keys = Gather("ctx", [text_own.at[0], text_own.at[1]], text_kv, *sems[9:12])
    moved = Weights(out_weight, patch_out, out_all, patch_all, *sems[12:])
    barrier(merge([image_job.partners(), image_keys.partners(), moved.partners()]))

    def heads(x_ref, q_ref, own, part):
        rows = slice(part * TILE, (part + 1) * TILE)
        squares = jnp.zeros((TILE, HD), F32)
        for i in range(32):
            piece = x_ref[i, 0, rows].astype(F32)
            squares += piece * piece
        scale = lax.rsqrt(jnp.sum(squares, axis=1, keepdims=True) * (1.0 / 4096.0) + EPSILON)
        normed = jnp.concatenate(
            [
                (x_ref[i, 0, rows].astype(F32) * scale * image_x[i, 0, UNIT : UNIT + 1].astype(F32)).astype(BF)
                for i in range(32)
            ],
            axis=1,
        )

        def head(weight, gain, factor):
            raw = jnp.dot(normed, weight, preferred_element_type=F32)
            mean = jnp.mean(raw * raw, axis=1, keepdims=True)
            return (raw * lax.rsqrt(mean + EPSILON) * gain * factor).astype(BF)

        own[0, rows] = head(wk_ref[...], kg_ref[...], 1.0)
        own[1, rows] = jnp.dot(normed, wv_ref[...], preferred_element_type=F32).astype(BF)
        q_ref[rows] = head(wq_ref[...], qg_ref[...], HD**-0.5)

    times = TIMES
    perform(
        image_job.events()
        + text_job.events(times[0])
        + [(times[1], lambda: heads(image_x, image_q, image_own, 0))]
        + [(times[1] + 1.0, lambda: heads(image_x, image_q, image_own, 1))]
        + image_keys.events(times[1] + 2.0)
        + [(times[2], lambda: heads(text_x, text_q, text_own, 0))]
        + [(times[2] + 1.0, lambda: heads(text_x, text_q, text_own, 1))]
        + text_keys.events(times[2] + 2.0)
        + moved.events(times[2] + 2.5)
    )


TIMES = (8.0, 26.0, 35.0)


def heads_of(image, text, wq, wk, wv, qg, kg, out_weight, patch_out):
    vmem = pl.BlockSpec(memory_space=pltpu.VMEM)
    rows = jax.ShapeDtypeStruct((UNIT, HD), BF)
    keys = jax.ShapeDtypeStruct((8, 2, UNIT, HD), BF)
    return pl.pallas_call(
        heads_kernel,
        out_shape=[
            rows,
            rows,
            keys,
            keys,
            jax.ShapeDtypeStruct((4, 8, HD, HD), BF),
            jax.ShapeDtypeStruct((8, HD, 512), BF),
        ],
        in_specs=[ANY, ANY] + [vmem] * 5 + [ANY, ANY],
        out_specs=[vmem, vmem] + [ANY] * 4,
        scratch_shapes=[
            pltpu.VMEM((32, 1) + image.shape, BF),
            pltpu.VMEM((32, 1) + text.shape, BF),
            pltpu.VMEM((2, UNIT, HD), BF),
            pltpu.VMEM((2, UNIT, HD), BF),
        ]
        + gather_sems("xz", 1)
        + gather_sems("xz", 1)
        + gather_sems("ctx", 2)
        + gather_sems("ctx", 2)
        + weight_sems(),
        compiler_params=pltpu.CompilerParams(
            collective_id=3, has_side_effects=True, vmem_limit_bytes=48 * 1024 * 1024
        ),
    )(image, text, wq, wk, wv, qg, kg, out_weight, patch_out)


MIX = 256


def mix_kernel(
    image, text, w_ref, image_stream, text_stream, image_out, text_out,
    blocks, outgoing, incoming, send, recv, local, part_send, part_recv,
):
    ctx, tile, mp = coordinates()
    units = blocks.shape[1]
    job = Gather("z", [image, text], blocks, send, recv, local)
    rings = [(mp + 1) % 4, (mp + 3) % 4, (mp + 2) % 4]
    barrier(merge([job.partners(), [(ctx, tile, rings[2])]]))

    def settle(u):
        for i, ring in enumerate(rings):
            dst = incoming.at[ring, u]
            remote(dst, dst, part_send.at[0, 0], part_recv.at[ring, u], (ctx, tile, ring)).wait_recv()
        stream, out, row = (image_stream, image_out, u * MIX) if u < 2 else (text_stream, text_out, u * MIX - UNIT)
        total = stream[row : row + MIX].astype(F32) + kept[u]
        for ring in rings:
            total = total + incoming[ring, u].astype(F32)
        out[row : row + MIX] = total.astype(BF)

    kept, copies = {}, []

    def multiply(u):
        x = jnp.concatenate([blocks[t, u] for t in range(8)], axis=1)
        for i, ring in enumerate(rings):
            outgoing[i, u] = jnp.dot(x, w_ref[ring], preferred_element_type=F32).astype(BF)
            copy = remote(
                outgoing.at[i, u], incoming.at[mp, u], part_send.at[i, u], part_recv.at[mp, u], (ctx, tile, ring)
            )
            copy.start()
            copies.append(copy)
        kept[u] = jnp.dot(x, w_ref[mp], preferred_element_type=F32)
        if u > 0:
            settle(u - 1)

    perform(job.column_events(multiply))
    settle(units - 1)
    job.close_column()
    for copy in copies:
        copy.wait_send()


def mix(image, text, w, image_stream, text_stream):
    dma = pltpu.SemaphoreType.DMA
    units = 2 * UNIT // MIX
    vmem = pl.BlockSpec(memory_space=pltpu.VMEM)
    return pl.pallas_call(
        mix_kernel,
        out_shape=[jax.ShapeDtypeStruct((UNIT, HD), BF)] * 2,
        in_specs=[ANY, ANY, vmem, vmem, vmem],
        out_specs=[vmem, vmem],
        scratch_shapes=[
            pltpu.VMEM((8, units, MIX, HD), BF),
            pltpu.VMEM((3, units, MIX, HD), BF),
            pltpu.VMEM((4, units, MIX, HD), BF),
        ]
        + gather_sems("z", units)
        + [dma((3, units)), dma((4, units))],
        compiler_params=pltpu.CompilerParams(
            collective_id=2, has_side_effects=True, vmem_limit_bytes=32 * 1024 * 1024
        ),
    )(image, text, w, image_stream, text_stream)


def up_kernel(
    image, text, w_ref, up_ref, work, cells_ref,
    blocks, product, terms, grid, above, below,
    work_send, work_recv, work_local,
    block_send, block_recv, twin_send, twin_recv, term_send, term_recv, grid_send, grid_recv, edge_send, edge_recv,
    own_sem,
):
    ctx, tile, mp = coordinates()
    z, core = tile // 2, tile % 2
    job = Gather("ctx", [image, text], work, work_send, work_recv, work_local)
    me = tile * 4 + mp
    group = []
    for i in range(1, 32):
        peer = (me + i) % 32
        group.append((ctx, peer // 4, peer % 4))
    barrier(merge([group, job.partners()]))
    rings = [(mp + 1) % 4, (mp + 3) % 4, (mp + 2) % 4]
    twin = (ctx, z * 2 + 1 - core, mp)
    own = core * 4 + mp
    copies = []

    def go(copy):
        copy.start()
        copies.append(copy)

    mine = [
        pltpu.make_async_copy(image, blocks.at[own], own_sem.at[0]),
        pltpu.make_async_copy(product.at[tile], terms.at[tile], own_sem.at[1]),
    ]
    tiles = [(tile + i) % 8 for i in (2, 6, 4, 1, 7, 3, 5)]
    down_edge = (mp == 3) & (tile < 7)
    up_edge = (mp == 0) & (tile > 0)
    down_copies = [
        lambda m=m: remote(
            grid.at[mp, :, pl.ds(16, 16)], above, edge_send.at[m], edge_recv.at[0], (ctx, (tile + 1) % 8, m)
        )
        for m in range(4)
    ]
    up_copies = [
        lambda m=m: remote(
            grid.at[mp, :, pl.ds(0, 16)], below, edge_send.at[m], edge_recv.at[1], (ctx, (tile + 7) % 8, m)
        )
        for m in range(4)
    ]

    def begin():
        for i, ring in enumerate(rings):
            go(remote(image, blocks.at[own], block_send.at[i], block_recv.at[mp], (ctx, tile, ring)))
        go(remote(image, blocks.at[own], twin_send.at[mp], twin_recv.at[mp], twin))
        mine[0].start()

    def pair(i):
        ring = rings[i]
        dst = blocks.at[core * 4 + ring]
        remote(dst, dst, block_send.at[0], block_recv.at[ring], (ctx, tile, ring)).wait_recv()
        go(remote(dst, dst, twin_send.at[ring], twin_recv.at[ring], twin))

    def multiply():
        mine[0].wait()
        for ring in range(4):
            dst = blocks.at[(1 - core) * 4 + ring]
            remote(dst, dst, twin_send.at[0], twin_recv.at[ring], twin).wait_recv()
        for s in range(2):
            x = jnp.concatenate([blocks[i, s * IMG_TOK : (s + 1) * IMG_TOK] for i in range(8)], axis=1)
            part = jnp.dot(x, w_ref[...].reshape(1024, 512), preferred_element_type=F32).astype(BF)
            product[:, s] = part.reshape(8, 32, 512)
        for i, t in enumerate(tiles):
            go(remote(product.at[t], terms.at[tile], term_send.at[i], term_recv.at[tile], (ctx, t, mp)))
        mine[1].start()

        @pl.when(tile == 0)
        def _():
            above[...] = jnp.zeros_like(above)

        @pl.when(tile == 7)
        def _():
            below[...] = jnp.zeros_like(below)

    def total():
        for t in tiles:
            dst = terms.at[t]
            remote(dst, dst, term_send.at[0], term_recv.at[t], (ctx, t, mp)).wait_recv()
        mine[1].wait()
        for c in range(2):
            total = terms[c].astype(F32)
            for k in range(1, 4):
                total = total + terms[2 * k + c].astype(F32)
            grid[mp, :, :, c * 512 : (c + 1) * 512] = silu(total).astype(BF)

        @pl.when(down_edge)
        def _():
            for make in down_copies:
                make().start()

        @pl.when(up_edge)
        def _():
            for make in up_copies:
                make().start()

        for i, ring in enumerate(rings):
            go(remote(grid.at[mp], grid.at[mp], grid_send.at[i], grid_recv.at[mp], (ctx, tile, ring)))

    def gathered():
        for ring in rings:
            dst = grid.at[ring]
            remote(dst, dst, grid_send.at[0], grid_recv.at[ring], (ctx, tile, ring)).wait_recv()

        @pl.when(tile > 0)
        def _():
            remote(above, above, edge_send.at[0], edge_recv.at[0], (ctx, tile, rings[0])).wait_recv()

        @pl.when(tile < 7)
        def _():
            remote(below, below, edge_send.at[0], edge_recv.at[1], (ctx, tile, rings[0])).wait_recv()

        convolve()

    def convolve():
        sums = [jnp.zeros((64, HD), F32) for _ in range(3)]
        for wr in range(6):
            for wc in range(6):
                pc = 3 if wc == 0 else 0 if wc == 5 else wc - 1
                lanes = slice(pc * CH, (pc + 1) * CH)
                if wr == 0:
                    a = jnp.concatenate([above[:, :, lanes], grid[3, :, 0:16, lanes]], axis=1)
                elif wr == 5:
                    a = jnp.concatenate([grid[0, :, 16:32, lanes], below[:, :, lanes]], axis=1)
                else:
                    a = grid[wr - 1, :, :, lanes]
                cell = wr * 6 + wc
                term = jnp.dot(
                    a.reshape(64, CH), up_ref[:, cell * HD : (cell + 1) * HD], preferred_element_type=F32
                )
                which = 0 if wc == 0 else 2 if wc == 5 else 1
                sums[which] = sums[which] + term
        column = lax.broadcasted_iota(jnp.int32, (64, HD), 0) % 16
        blank = jnp.zeros((1, HD), F32)
        from_left = jnp.concatenate([blank, sums[0][:63]], axis=0)
        from_right = jnp.concatenate([sums[2][1:], blank], axis=0)
        cells_ref[...] = (
            sums[1] + jnp.where(column == 0, 0.0, from_left) + jnp.where(column == 15, 0.0, from_right)
        )

    perform(
        job.events()
        + [(0.0, begin), (6.0, lambda: pair(0)), (6.0, lambda: pair(1)), (8.0, lambda: pair(2))]
        + [(10.0, multiply), (24.0, total), (32.0, gathered)]
    )
    for copy in copies:
        copy.wait_send()

    @pl.when(down_edge)
    def _():
        for make in down_copies:
            make().wait_send()

    @pl.when(up_edge)
    def _():
        for make in up_copies:
            make().wait_send()


def up_block(image, text, w, up_w):
    dma = pltpu.SemaphoreType.DMA
    vmem = pl.BlockSpec(memory_space=pltpu.VMEM)
    work = jax.ShapeDtypeStruct((8, 2, UNIT, HD), BF)
    return pl.pallas_call(
        up_kernel,
        out_shape=[work, jax.ShapeDtypeStruct((64, HD), F32)],
        in_specs=[ANY, ANY, vmem, vmem],
        out_specs=[ANY, vmem],
        scratch_shapes=[
            pltpu.VMEM((8, UNIT, HD), BF),
            pltpu.VMEM((8, 2, 32, 512), BF),
            pltpu.VMEM((8, 2, 32, 512), BF),
            pltpu.VMEM((4, 2, 32, 1024), BF),
            pltpu.VMEM((2, 16, 1024), BF),
            pltpu.VMEM((2, 16, 1024), BF),
        ]
        + gather_sems("ctx", 2)
        + [dma((n,)) for n in (3, 4, 4, 4, 7, 8, 3, 4, 4, 2, 2)],
        compiler_params=pltpu.CompilerParams(
            collective_id=6, has_side_effects=True, vmem_limit_bytes=32 * 1024 * 1024
        ),
    )(image, text, w, up_w)


def attention_kernel(top_ref, slot_ref, q_ref, lim_t_ref, lim_i_ref, text_ref, image_ref, out_ref):
    tile = pl.program_id(0)
    q = q_ref[...]
    cols = lax.broadcasted_iota(jnp.int32, (TILE, 1024), 1)

    def step(carry, k, v, limit):
        top, total, acc = carry
        s = lax.dot_general(q, k, (((1,), (1,)), ((), ())), preferred_element_type=F32)
        s = jnp.where(cols < limit, s, NEGATIVE)
        new = jnp.maximum(top, jnp.max(s, axis=1, keepdims=True))
        w = jnp.exp(s - new)
        factor = jnp.exp(top - new)
        total = total * factor + jnp.sum(w, axis=1, keepdims=True)
        acc = acc * factor + jnp.dot(w.astype(BF), v, preferred_element_type=F32)
        return new, total, acc

    def text_step(n, carry):
        k = jnp.concatenate([text_ref[2 * n, 0], text_ref[2 * n + 1, 0]], axis=0)
        v = jnp.concatenate([text_ref[2 * n, 1], text_ref[2 * n + 1, 1]], axis=0)
        return step(carry, k, v, lim_t_ref[...] - n * 1024)

    def image_step(n, carry):
        ks, vs = [], []
        for u in range(4):
            slot = slot_ref[n * 4 + u]
            rows = pl.ds(pl.multiple_of((slot % 2) * IMG_TOK, IMG_TOK), IMG_TOK)
            ks.append(image_ref[slot // 2, 0, rows])
            vs.append(image_ref[slot // 2, 1, rows])
        return step(carry, jnp.concatenate(ks, axis=0), jnp.concatenate(vs, axis=0), lim_i_ref[...] - n * 1024)

    carry = (jnp.full((TILE, 1), NEGATIVE, F32), jnp.zeros((TILE, 1), F32), jnp.zeros((TILE, HD), F32))
    carry = lax.fori_loop(0, (top_ref[1, tile] + 1023) // 1024, image_step, carry)
    carry = lax.fori_loop(0, (top_ref[0, tile] + 1023) // 1024, text_step, carry)
    _, total, acc = carry
    out_ref[...] = (acc / total).astype(BF)


def attention(slots, q, lim_t, lim_i, text, image):
    rows = q.shape[0]
    tops = jnp.stack([jnp.max(lim_t.reshape(-1, TILE), axis=1), jnp.max(lim_i.reshape(-1, TILE), axis=1)])
    whole = pl.BlockSpec((8, 2, UNIT, HD), lambda i, *_: (0, 0, 0, 0))
    grid_spec = pltpu.PrefetchScalarGridSpec(
        num_scalar_prefetch=2,
        grid=(rows // TILE,),
        in_specs=[
            pl.BlockSpec((TILE, HD), lambda i, *_: (i, 0)),
            pl.BlockSpec((TILE, 1), lambda i, *_: (i, 0)),
            pl.BlockSpec((TILE, 1), lambda i, *_: (i, 0)),
            whole,
            whole,
        ],
        out_specs=pl.BlockSpec((TILE, HD), lambda i, *_: (i, 0)),
    )
    return pl.pallas_call(
        attention_kernel,
        grid_spec=grid_spec,
        out_shape=jax.ShapeDtypeStruct((rows, HD), BF),
        compiler_params=pltpu.CompilerParams(vmem_limit_bytes=48 * 1024 * 1024),
    )(tops, slots, q, lim_t[:, None], lim_i[:, None], text, image)


def window_pairs(latents):
    wide = jnp.pad(latents, ((0, 0), (0, 0), (8, 32)))
    before = wide[..., 0:512].reshape(2, 8, 16, 32)[..., :8]
    middle = latents.reshape(2, 8, 16, 32)
    after = wide[..., 40:552].reshape(2, 8, 16, 32)[..., :8]
    joined = jnp.concatenate([before, middle, after], axis=-1)
    return jnp.concatenate([joined[:, 0::2], joined[:, 1::2], jnp.zeros((2, 4, 16, 32), BF)], axis=-1)


def up_weights(up_conv):
    taps = up_conv.reshape(9, CH, CIN).transpose(1, 0, 2).reshape(CH, 72)
    row = lax.broadcasted_iota(jnp.int32, (72, 36 * HD), 0)
    col = lax.broadcasted_iota(jnp.int32, (72, 36 * HD), 1)
    cell, inner = col // HD, col % HD
    a, b = cell // 6 - inner // 32, cell % 6 - (inner // 8) % 4
    inside = (a >= 0) & (a <= 2) & (b >= 0) & (b <= 2)
    pick = jnp.where(inside & (row == (a * 3 + b) * 8 + inner % 8), 1.0, 0.0).astype(BF)
    return jnp.dot(taps, pick, preferred_element_type=F32).astype(BF)


def shards(
    text_embed,
    latents,
    down_conv,
    patch_in,
    norm_gain,
    query_weight,
    key_weight,
    value_weight,
    query_gain,
    key_gain,
    out_weight,
    patch_out,
    up_conv,
    span_start,
    image_of_slot,
):
    ctx = lax.axis_index("ctx")
    images = jnp.arange(16, dtype=jnp.int32)
    before = span_start - images * IMG_TOK
    is_slot = image_of_slot[None, :] == images[:, None]
    slot_of = jnp.sum(jnp.where(is_slot, images[None, :], 0), axis=1)

    mp = lax.axis_index("mp")
    channels = jnp.arange(CH, dtype=jnp.int32)[None, :] // 64 == mp
    down = jnp.where(channels, jnp.tile(down_conv, (1, 4)), 0)
    image, text_all = opening(
        window_pairs(latents), jnp.pad(down, ((0, 8), (0, 0))), text_embed, patch_in, norm_gain[None, :]
    )

    text_rows = ctx * UNIT + jnp.arange(UNIT, dtype=jnp.int32)
    seen = jnp.sum((before[None, :] <= text_rows[:, None]).astype(jnp.int32), axis=1)
    text = jnp.take(text_all.reshape(8192, HD), text_rows + IMG_TOK * seen, axis=0, mode="clip")
    image_q, text_q, image_kv, text_kv, out_all, patch_all = heads_of(
        image, text, query_weight, key_weight, value_weight, query_gain.reshape(1, HD), key_gain.reshape(1, HD),
        out_weight.reshape(8, 4, HD, HD), patch_out,
    )

    slots = ctx * 2 + jnp.arange(2, dtype=jnp.int32)
    here = slots[:, None] == images[None, :]
    own_image = jnp.sum(jnp.where(here, image_of_slot[None, :], 0), axis=1)
    own_before = jnp.sum(jnp.where(own_image[:, None] == images[None, :], before[None, :], 0), axis=1)
    spread = lambda pair: jnp.broadcast_to(pair[:, None], (2, IMG_TOK)).reshape(UNIT)
    image_mix = attention(
        slot_of, image_q, spread(own_before), spread((own_image + 1) * IMG_TOK), text_kv, image_kv
    )
    text_mix = attention(slot_of, text_q, text_rows + 1, seen * IMG_TOK, text_kv, image_kv)

    image_out, text_out = mix(image_mix, text_mix, out_all.reshape(4, 1024, HD), image, text)
    work, cells = up_block(image_out, text_out, patch_all, up_weights(up_conv))
    noise_pred = cells.reshape(2, 2, 16, 4, 32).transpose(0, 1, 3, 2, 4).reshape(2, 8, 512)

    positions = ctx * 1024 + jnp.arange(1024, dtype=jnp.int32)
    started = (span_start[None, :] <= positions[:, None]).astype(jnp.int32)
    passed = jnp.sum((span_start[None, :] + IMG_TOK <= positions[:, None]).astype(jnp.int32), axis=1)
    inside = jnp.sum(started, axis=1) > passed
    now = passed[:, None] == images[None, :]
    slot = jnp.sum(jnp.where(now, slot_of[None, :], 0), axis=1)
    start = jnp.sum(jnp.where(now, span_start[None, :], 0), axis=1)
    row = positions - passed * IMG_TOK
    text_source = row // UNIT * 1024 + UNIT + row % UNIT
    image_source = slot // 2 * 1024 + slot % 2 * IMG_TOK + positions - start
    source = jnp.where(inside, image_source, text_source)
    layer_out = jnp.take(work.reshape(8192, HD), source, axis=0, mode="clip")
    return layer_out, noise_pred


def solution(mesh):
    return jax.shard_map(
        shards,
        mesh=mesh,
        in_specs=(
            P("ctx", ("tile", "mp")),
            P("ctx", "tile", None),
            P(None, "mp"),
            P(None, ("tile", "mp")),
            P(("tile", "mp")),
            P(None, ("tile", "mp")),
            P(None, ("tile", "mp")),
            P(None, ("tile", "mp")),
            P(),
            P(),
            P(None, ("tile", "mp")),
            P(("tile", "mp"), None),
            P(),
            P(),
            P(),
        ),
        out_specs=(P("ctx", ("tile", "mp")), P("ctx", "tile", None)),
        check_vma=False,
    )
```

time: 320 us -> 260 us (0.81)
  Pallas kernels: 282 us -> 231 us
  local copies, waits for them, and re-layouts: 29.2 us -> 22.6 us
    pallas_call x8 -> x3, Pallas kernels: 232 us -> 181 us  [the longest x1 84.6 us: heads_of(): pl.pallas_call(heads_kernel, out_shape=[rows, rows, keys, keys, jax.Shape...]
    gather x2 -> x1, local copies, waits for them, and re-layouts: 6.41 us -> 4.31 us  [shards(): layer_out = jnp.take(work.reshape(8192, HD), source, axis=0, mode='clip')]
    unnamed x59 -> x47, local copies, waits for them, and re-layouts: 13.5 us -> 12.2 us
where the time goes in v3:
time: 260 us; the launch traced here: 259 us
  Pallas kernels  231 us (89%)
  local copies, waits for them, and re-layouts  22.6 us (9%)
  other arithmetic  2.69 us (1%)
    pallas_call x1, Pallas kernels, heads_of(): pl.pallas_call(heads_kernel, out_shape=[rows, rows, keys, keys, jax.Shape...  84.6 us
    pallas_call x1, Pallas kernels, up_block(): pl.pallas_call(up_kernel, out_shape=[work, jax.ShapeDtypeStruct((64, HD),...  55.8 us
    pallas_call x1, Pallas kernels, opening(): pl.pallas_call(opening_kernel, out_shape=[jax.ShapeDtypeStruct((UNIT + 32...  40.9 us
    pallas_call x1, Pallas kernels, mix(): pl.pallas_call(mix_kernel, out_shape=[jax.ShapeDtypeStruct((UNIT, HD), BF...  38.6 us
    unnamed x47, local copies, waits for them, and re-layouts  12.2 us
    pallas_call x2, Pallas kernels, attention(): pl.pallas_call(attention_kernel, grid_spec=grid_spec, out_shape=jax.Shape...  10.8 us

profile of v3, /device:TPU:1, one launch (start us, length us, event | category | flops | bytes accessed | tf_op | source)
XLA Modules:
  0.0 258.7 jit_solution(16541491422329453376)
XLA Ops:
  0.7 0.8 broadcast_add_fusion.1
  1.9 0.9 pad_slice_fusion.1
  3.0 0.8 reshape.331
  4.5 40.9 %shard_map.158 = (bf16[544,128]{1,0:T(8,128)(2,1)S(1)}, bf16[8,2,512,128]{3,2,1,0:T(8,128)(2,1)S(1)}) custom-call(bf16[2,4,16,128]{3,2,1,0:T(8,128)(2,1)S(1)} %maximum_maximum_fusion.pairs, bf16[80,256]{1,0:T(8,128)(2,1)S(1)} %pad.9.down, bf16[1024,128]{1,0:T(8,128)(2,1)S(1)} %copy-done.14, bf16[4096,128]{1,0:T(8,128)(2,1)S(1)} %copy-done.7, ...), custom_call_target="tpu_custom_call" | custom-call | tf_op jit(solution)/shard_map/pallas_call | solution.py:402
  45.4 1.3 copy-done.13
  46.7 2.9 %gather_fusion = bf16[512,128]{1,0:T(8,128)(2,1)S(1)} fusion(bf16[8192,128]{1,0:T(8,128)(2,1)} %bitcast.44, s32[1024]{0:T(1024)S(1)} %pad_clamp_fusion), kind=kCustom, calls=%fused_computation | custom fusion | bytes 264192 | tf_op jit(solution)/shard_map/jit(_take)/gather | solution.py:881
  49.7 1.2 copy-done.10
  50.9 1.2 copy-done.11
  52.1 1.2 copy-done.12
  53.4 84.6 %shard_map.159 = (bf16[512,128]{1,0:T(8,128)(2,1)S(1)}, bf16[512,128]{1,0:T(8,128)(2,1)S(1)}, bf16[8,2,512,128]{3,2,1,0:T(8,128)(2,1)}, bf16[8,2,512,128]{3,2,1,...) custom-call(bf16[544,128]{1,0:T(8,128)(2,1)S(1)} %get-tuple-element.14.image.image_stream, ...), custom_call_target="tpu_custom_call" | custom-call | tf_op jit(solution)/shard_map/pallas_call | solution.py:485
  138.0 1.0 copy-done.5
  139.0 1.0 copy-done.8
  140.4 1.6 copy-done.1
  142.0 1.6 copy-done.3
  143.6 4.3 %shard_map.161.text = bf16[512,128]{1,0:T(8,128)(2,1)S(1)} custom-call(s32[2,2]{1,0:T(2,128)S(1)} %pad_add_fusion.1.top_ref, s32[16]{0:T(128)S(1)} %select_reduce_fusion.2.slot_ref, bf16[512,128]{1,0:T(8,128)(2,1)S(1)} %get-tuple-element.19.q_ref, s32[512,1]{1,0:T(8,128)S(1)} %get-tuple-element.41.lim_t_ref, s32[512,1]{1,0:T(8,128)S(1)} %copy.28.lim_i_ref, ...), custom_call_target="tpu_custom_call" | custom-call | tf_op jit(solution)/shard_map/pallas_call | solution.py:821
  148.1 0.2 fusion.51
  148.3 0.2 broadcast_bitcast_fusion.1
  149.0 1.6 copy-done.4
  150.6 6.5 %shard_map.160.image = bf16[512,128]{1,0:T(8,128)(2,1)S(1)} custom-call(s32[2,2]{1,0:T(2,128)S(1)} %pad_add_fusion.top_ref, s32[16]{0:T(128)S(1)} %select_reduce_fusion.2.slot_ref, bf16[512,128]{1,0:T(8,128)(2,1)S(1)} %get-tuple-element.16.q_ref, s32[512,1]{1,0:T(8,128)S(1)} %bitcast.41, s32[512,1]{1,0:T(8,128)S(1)} %bitcast.42, ...), custom_call_target="tpu_custom_call" | custom-call | tf_op jit(solution)/shard_map/pallas_call | solution.py:821
  157.1 38.6 %shard_map.162 = (bf16[512,128]{1,0:T(8,128)(2,1)S(1)}, bf16[512,128]{1,0:T(8,128)(2,1)S(1)}) custom-call(bf16[512,128]{1,0:T(8,128)(2,1)S(1)} %shard_map.160.image, bf16[512,128]{1,0:T(8,128)(2,1)S(1)} %shard_map.161.text, bf16[4,1024,128]{2,1,0:T(8,128)(2,1)S(1)} %bitcast.43, bf16[544,128]{1,0:T(8,128)(2,1)S(1)} %get-tuple-element.14.image.image_stream, ...), custom_call_target="tpu_custom_call" | custom-call | tf_op jit(solution)/shard_map/pallas_call | solution.py:563
  195.8 1.5 fusion.up_ref
  197.3 55.8 %shard_map.163 = (bf16[8,2,512,128]{3,2,1,0:T(8,128)(2,1)S(1)}, f32[64,128]{1,0:T(8,128)S(1)}) custom-call(bf16[512,128]{1,0:T(8,128)(2,1)S(1)} %get-tuple-element.21.image, bf16[512,128]{1,0:T(8,128)(2,1)S(1)} %get-tuple-element.22.text, bf16[8,128,512]{2,1,0:T(8,128)(2,1)S(1)} %copy-done.6, bf16[256,4608]{1,0:T(8,128)(2,1)S(1)} %fusion.up_ref), custom_call_target="tpu_custom_call" | custom-call | tf_op jit(solution)/shard_map/pallas_call | solution.py:747
  253.5 4.3 %gather_fusion.1 = bf16[1024,128]{1,0:T(8,128)(2,1)} fusion(bf16[8192,128]{1,0:T(8,128)(2,1)S(1)} %bitcast.40, s32[1024]{0:T(1024)S(1)} %broadcast_clamp_fusion), kind=kCustom, calls=%fused_computation.1 | custom fusion | bytes 528384 | tf_op jit(solution)/shard_map/jit(_take)/gather | solution.py:912
  258.0 0.7 reshape.342
  (78 shorter events, 2.7 us)
Async XLA Ops:
  0.6 195.2 %copy-start = (bf16[2304,8]{0,1:T(8,128)(2,1)S(1)}, bf16[2304,8]{0,1:T(8,128)(2,1)}, u32[]{:S(2)}) copy-start(bf16[2304,8]{0,1:T(8,128)(2,1)} %param.27) | copy-start | bytes 110596
  0.6 3.5 %copy-start.18 = (bf16[72,64]{0,1:T(8,128)(2,1)S(1)}, bf16[72,64]{0,1:T(8,128)(2,1)}, u32[]{:S(2)}) copy-start(bf16[72,64]{0,1:T(8,128)(2,1)} %param.17) | copy-start | bytes 27652
  0.7 3.8 %copy-start.15 = (bf16[128]{0:T(256)(128)(2,1)S(1)}, bf16[128]{0:T(256)(128)(2,1)}, u32[]{:S(2)}) copy-start(bf16[128]{0:T(256)(128)(2,1)} %param.19) | copy-start | bytes 772
  0.7 3.8 %copy-start.14 = (bf16[1024,128]{1,0:T(8,128)(2,1)S(1)}, bf16[1024,128]{1,0:T(8,128)(2,1)}, u32[]{:S(2)}) copy-start(bf16[1024,128]{1,0:T(8,128)(2,1)} %text.1) | copy-start | bytes 786436
  0.7 3.8 %copy-start.7 = (bf16[4096,128]{1,0:T(8,128)(2,1)S(1)}, bf16[4096,128]{1,0:T(8,128)(2,1)}, u32[]{:S(2)}) copy-start(bf16[4096,128]{1,0:T(8,128)(2,1)} %patch_ref.1) | copy-start | bytes 3145732
  4.4 45.2 %copy-start.16 = (f32[128]{0:T(128)S(1)}, f32[128]{0:T(128)}, u32[]{:S(2)}) copy-start(f32[128]{0:T(128)} %param.23) | copy-start | bytes 1540
  4.4 45.2 %copy-start.17 = (f32[128]{0:T(128)S(1)}, f32[128]{0:T(128)}, u32[]{:S(2)}) copy-start(f32[128]{0:T(128)} %param.24) | copy-start | bytes 1540
  45.4 1.4 copy-start.13
  49.7 1.2 copy-start.10
  50.9 1.2 copy-start.11
  52.1 1.2 copy-start.12
  53.4 86.9 %copy-start.20 = (s32[16]{0:T(128)S(1)}, s32[16]{0:T(128)}, u32[]{:S(2)}) copy-start(s32[16]{0:T(128)} %param.29) | copy-start | bytes 196
  138.0 1.0 copy-start.5
  139.0 1.0 copy-start.8
  140.4 1.6 copy-start.1
  142.0 1.6 copy-start.3
  143.6 5.4 %copy-start.2 = (bf16[8,2,512,128]{3,2,1,0:T(8,128)(2,1)S(1)}, bf16[8,2,512,128]{3,2,1,0:T(8,128)(2,1)}, u32[]{:S(2)}) copy-start(bf16[8,2,512,128]{3,2,1,0:T(8,128)(2,1)} %get-tuple-element.18.image_ref) | copy-start | bytes 6291460
  149.0 1.6 copy-start.4
  150.6 6.5 %copy-start.9 = (bf16[4,8,128,128]{3,2,1,0:T(8,128)(2,1)S(1)}, bf16[4,8,128,128]{3,2,1,0:T(8,128)(2,1)}, u32[]{:S(2)}) copy-start(bf16[4,8,128,128]{3,2,1,0:T(8,128)(2,1)} %copy-done.8) | copy-start | bytes 3145732
  195.8 1.5 copy-start.6
  197.3 55.9 %copy-start.19 = (s32[16]{0:T(128)S(1)}, s32[16]{0:T(128)}, u32[]{:S(2)}) copy-start(s32[16]{0:T(128)} %param.28) | copy-start | bytes 196
